TPU v7x, 32 devices: a whole 2x2x4 slice. The times are simulated.
32 devices in a mesh: grp: 2 (over y), row: 4 (over z), col: 2 (over x), pair: 2 (over core).
Axes of the slice: x: 2, y: 2, z: 4, core: 2. Of those that a mesh axis runs over, the one named last changes fastest.
Arguments:
- features_in: bfloat16 [128, 32, 512], P('grp', 'row', ('col', 'pair')), parts along dimension 0, may hold values from -8 to 8
- filters_one: bfloat16 [64, 3, 3, 64], replicated, may hold values from -0.25 to 0.25
- filters_two: bfloat16 [512, 3, 3, 256], P('row'), may hold values from -0.125 to 0.125
- out_grad: bfloat16 [1024, 128, 8], P(('grp', 'row'), ('col', 'pair')), parts along dimension 0, may hold values from -24 to 24
Outputs:
- input_grad: bfloat16 [128, 32, 512], P('grp', 'row', ('col', 'pair')), parts along dimension 0
- grad_one: float32 [128, 3, 3, 64], P('grp'), parts along dimension 0
- grad_two: float32 [1024, 3, 3, 256], P(('grp', 'row')), parts along dimension 0
There are 2 independent parts, one for each index of `grp`. A program takes and returns all parts, laid end to end along the dimension named above; an argument that names none is the same for every part. Nothing has to cross between parts.
All inputs are finite; a program needn't handle non-finite values.
Results may differ from a plain program's by a relative error of at most 0.015.
Values may be sent and summed in bfloat16 or wider, within the bound.
A program may use at most 64 MiB of HBM per device.

v0:
```python
import functools
import math

import jax
import jax.numpy as jnp
from jax import lax
from jax.experimental import pallas as pl
from jax.experimental.pallas import tpu as pltpu
from jax.sharding import PartitionSpec as P

MESH = pl.DeviceIdType.MESH
VMEM = pl.BlockSpec(memory_space=pltpu.VMEM)
STRIP = ("col", "pair")


def place():
    return lax.axis_index("row"), lax.axis_index(STRIP)


def device_at(row, strip):
    pairs = lax.axis_size("pair")
    return (lax.axis_index("grp"), row, lax.div(strip, pairs), lax.rem(strip, pairs))


def params(number):
    share = max(1, lax.axis_size("row") * lax.axis_size(STRIP) // 64)
    return pltpu.CompilerParams(
        collective_id=number, has_side_effects=True, vmem_limit_bytes=share * 24 * 1024 * 1024
    )


WAYS = [(a, b) for a in (-1, 0, 1) for b in (-1, 0, 1) if (a, b) != (0, 0)]


def first_kernel(
    rows, strips, cells, edge_up, kernel, pick_cols, spread_lanes,
    got_up, pre, gathered, shifted, near, block, send_sem, recv_sem, row_send, row_recv,
):
    row, strip = place()
    band, channels, width = cells.shape
    band2 = band // 4
    lanes = [pl.ds(0, width), pl.ds(width, width), pl.ds(2 * width, width)]
    tops = [pl.ds(0, 2), pl.ds(2, band), pl.ds(band + 2, 2)]

    def there(way):
        a, b = row + way[0], strip + way[1]
        return (a >= 0) & (a < rows) & (b >= 0) & (b < strips)

    barrier = pltpu.get_barrier_semaphore()
    for way in WAYS:
        if way[1] != 0:
            @pl.when(there(way))
            def _(way=way):
                pl.semaphore_signal(
                    barrier, inc=1, device_id=device_at(row + way[0], strip + way[1]), device_id_type=MESH
                )
    _, _, row_device = group("rows")
    for step in range(1, rows):
        pl.semaphore_signal(
            barrier, inc=1, device_id=row_device(lax.rem(row + step, rows)), device_id_type=MESH
        )

    def landing(way):
        return near.at[tops[way[0] + 1], :, lanes[way[1] + 1]]

    for way in WAYS:
        @pl.when(jnp.logical_not(there(way)))
        def _(way=way):
            slot = landing(way)
            slot[...] = jnp.zeros(slot.shape, slot.dtype)
            if way[0] == 0:
                slot = got_up.at[0 if way[1] < 0 else 1]
                slot[...] = jnp.zeros(slot.shape, slot.dtype)
    near[tops[1], :, lanes[1]] = cells[...]

    high = 1 + jnp.where(row > 0, 1, 0) + jnp.where(row < rows - 1, 1, 0)
    across = jnp.where(strip > 0, 1, 0) + jnp.where(strip < strips - 1, 1, 0)
    pl.semaphore_wait(barrier, high * across + rows - 1)

    def copy_to(way):
        back = (-way[0], -way[1])
        source = cells.at[[pl.ds(0, 2), pl.ds(0, band), pl.ds(band - 2, 2)][way[0] + 1]]
        return pltpu.make_async_remote_copy(
            src_ref=source,
            dst_ref=landing(back),
            send_sem=send_sem.at[WAYS.index(way)],
            recv_sem=recv_sem.at[WAYS.index(back)],
            device_id=device_at(row + way[0], strip + way[1]),
            device_id_type=MESH,
        )

    def upstream_to(way):
        side = 0 if way[1] < 0 else 1
        return pltpu.make_async_remote_copy(
            src_ref=edge_up.at[side],
            dst_ref=got_up.at[1 - side],
            send_sem=send_sem.at[8 + side],
            recv_sem=recv_sem.at[9 - side],
            device_id=device_at(row, strip + way[1]),
            device_id_type=MESH,
        )

    def arrival(way):
        back = (-way[0], -way[1])
        return pltpu.make_async_remote_copy(
            src_ref=landing(way),
            dst_ref=landing(way),
            send_sem=send_sem.at[WAYS.index(way)],
            recv_sem=recv_sem.at[WAYS.index(way)],
            device_id=device_at(row + back[0], strip + back[1]),
            device_id_type=MESH,
        )

    for way in sorted(WAYS, key=lambda w: (abs(w[0]), -abs(w[1]))):
        @pl.when(there(way))
        def _(way=way):
            copy_to(way).start()
    for way in ((0, -1), (0, 1)):
        @pl.when(there(way))
        def _(way=way):
            upstream_to(way).start()
    for way in WAYS:
        @pl.when(there(way))
        def _(way=way):
            arrival(way).wait_recv()

    full = 3 * width

    @pl.loop(0, band + 4)
    def _(h):
        here = near[h]
        wide = here.astype(jnp.float32)
        shifted[h, pl.ds(0, channels)] = pltpu.roll(wide, 1, 1).astype(jnp.bfloat16)
        shifted[h, pl.ds(channels, channels)] = here
        shifted[h, pl.ds(2 * channels, channels)] = pltpu.roll(wide, full - 1, 1).astype(jnp.bfloat16)

    @pl.loop(0, band + 2)
    def _(h):
        patches = shifted[pl.ds(h, 3)].reshape(9 * channels, full)
        pre[h] = jnp.dot(kernel[...], patches, preferred_element_type=jnp.float32)

    def silu(values):
        return values / (1.0 + jnp.exp(-values))

    contract = (((1,), (1,)), ((), ()))
    room = pick_cols.shape[0] // 2
    pooled = []
    for u in range(band2):
        total = jnp.zeros((room, 4 * channels), jnp.float32)
        for i in range(2):
            at = 1 + 4 * u + 2 * i
            pair_sum = (silu(pre[at]) + silu(pre[at + 1])) * 0.25
            upper = pair_sum.astype(jnp.bfloat16)
            lower = (pair_sum - upper.astype(jnp.float32)).astype(jnp.bfloat16)
            mean = lax.dot_general(pick_cols[...], upper, contract, preferred_element_type=jnp.float32)
            mean += lax.dot_general(pick_cols[...], lower, contract, preferred_element_type=jnp.float32)
            mean = mean.astype(jnp.bfloat16)
            for j in range(2):
                total += jnp.dot(
                    mean[j * room : (j + 1) * room],
                    spread_lanes[2 * i + j],
                    preferred_element_type=jnp.float32,
                )
        pooled.append(total)
    pooled = jnp.concatenate(pooled, 0).astype(jnp.bfloat16)
    block[...] = pooled
    finish = post(rows, row, row_device, lambda peer: block, gathered, row_send, row_recv)
    gathered[row] = pooled
    for way in WAYS:
        @pl.when(there(way))
        def _(way=way):
            copy_to(way).wait_send()
            if way[0] == 0:
                upstream_to(way).wait_send()
                upstream_to((-way[0], -way[1])).wait_recv()
    finish()


def first_layer(features_in, upstream, filters_one, number):
    channels, band, width = features_in.shape
    rows, strips = lax.axis_size("row"), lax.axis_size(STRIP)
    strip = lax.axis_index(STRIP)
    band2, width2 = band // 4, width // 4
    quads = 4 * channels
    near2 = width2 + 6
    room = -(-near2 // 16) * 16
    if (band2 * (-(-near2 // 8) * 8)) % 16 == 0:
        room = -(-near2 // 8) * 8
    height2, _, filters = upstream.shape
    cells = jnp.transpose(features_in, (1, 0, 2))
    edge_up = jnp.stack(
        [upstream[:, :2].reshape(2 * height2, filters), upstream[:, -2:].reshape(2 * height2, filters)]
    )
    v = jnp.arange(room)
    start = width + 4 * (v - 3)[None, :, None] + 2 * jnp.arange(2)[:, None, None]
    lane = jnp.arange(3 * width)[None, None, :]
    at_col = strip * width2 - 3 + v
    inside = (v < near2) & (at_col >= 0) & (at_col < width2 * strips)
    pick_cols = ((lane == start) | (lane == start + 1)) & inside[None, :, None]
    pick_cols = pick_cols.astype(jnp.bfloat16).reshape(2 * room, 3 * width)
    target = 4 * jnp.arange(channels)[None, :, None] + jnp.arange(4)[:, None, None]
    spread_lanes = (jnp.arange(quads)[None, None] == target).astype(jnp.bfloat16)
    got_up, pre, gathered, shifted = pl.pallas_call(
        functools.partial(first_kernel, rows, strips),
        out_shape=(
            jax.ShapeDtypeStruct(edge_up.shape, jnp.bfloat16),
            jax.ShapeDtypeStruct((band + 2, channels, 3 * width), jnp.float32),
            jax.ShapeDtypeStruct((rows, band2 * room, quads), jnp.bfloat16),
            jax.ShapeDtypeStruct((band + 4, 3 * channels, 3 * width), jnp.bfloat16),
        ),
        in_specs=[VMEM] * 5,
        out_specs=(VMEM,) * 4,
        scratch_shapes=[
            pltpu.VMEM((band + 4, channels, 3 * width), jnp.bfloat16),
            pltpu.VMEM((band2 * room, quads), jnp.bfloat16),
        ]
        + sems(10)
        + sems(rows),
        compiler_params=params(number),
    )(cells, edge_up, filters_one.reshape(channels, 9 * channels), pick_cols, spread_lanes)
    own = gathered.reshape(rows * band2, room, quads)[:, :near2]
    got_up = got_up.reshape(2, height2, 2, filters)
    inner = slice(width - 1, 2 * width + 1)
    return (
        shifted,
        pre[:, :, inner],
        own,
        jnp.concatenate([got_up[0], upstream, got_up[1]], 1),
    )


def post(count, me, device_of, source, landing, send_sem, recv_sem):
    def copy_of(step):
        peer = lax.rem(me + step, count)
        return pltpu.make_async_remote_copy(
            src_ref=source(peer),
            dst_ref=landing.at[me],
            send_sem=send_sem.at[step],
            recv_sem=recv_sem.at[me],
            device_id=device_of(peer),
            device_id_type=MESH,
        )

    def arrival(step):
        peer = lax.rem(me + step, count)
        return pltpu.make_async_remote_copy(
            src_ref=source(peer),
            dst_ref=landing.at[peer],
            send_sem=send_sem.at[step],
            recv_sem=recv_sem.at[peer],
            device_id=device_of(peer),
            device_id_type=MESH,
        )

    @pl.loop(1, count)
    def _(step):
        copy_of(step).start()

    def finish():
        @pl.loop(1, count)
        def _(step):
            copy_of(step).wait_send()
            arrival(step).wait_recv()

    return finish


def group(kind):
    rows, strips = lax.axis_size("row"), lax.axis_size(STRIP)
    row, strip = place()
    if kind == "all":
        return (
            rows * strips,
            row * strips + strip,
            lambda i: device_at(lax.div(i, strips), lax.rem(i, strips)),
        )
    if kind == "strips":
        return strips, strip, lambda i: device_at(row, i)
    return rows, row, lambda i: device_at(i, strip)


def sems(count):
    return [pltpu.SemaphoreType.DMA((count,)), pltpu.SemaphoreType.DMA((count,))]


def group_size(kind):
    rows, strips = lax.axis_size("row"), lax.axis_size(STRIP)
    return dict(all=rows * strips, strips=strips, rows=rows)[kind]


def total_of(count, landing):
    return lax.fori_loop(
        1,
        count,
        lambda i, value: value + landing[i].astype(jnp.float32),
        landing[0].astype(jnp.float32),
    )


def scatter_kernel(
    blocks, strip_map, out, maps, landing, send_sem, recv_sem, map_send, map_recv, on_send
):
    rows, me, row_device = group("rows")
    row, strip = place()
    cols, pairs = lax.axis_size("col"), lax.axis_size("pair")
    col, pair = lax.axis_index("col"), lax.axis_index("pair")

    barrier = pltpu.get_barrier_semaphore()
    for step in range(1, rows):
        pl.semaphore_signal(
            barrier, inc=1, device_id=row_device(lax.rem(me + step, rows)), device_id_type=MESH
        )
    for step in range(1, cols):
        pl.semaphore_signal(
            barrier,
            inc=1,
            device_id=device_at(row, lax.rem(col + step, cols) * pairs + pair),
            device_id_type=MESH,
        )
    for step in range(1, pairs):
        pl.semaphore_signal(
            barrier,
            inc=1,
            device_id=device_at(row, col * pairs + lax.rem(pair + step, pairs)),
            device_id_type=MESH,
        )
    pl.semaphore_wait(barrier, rows + cols + pairs - 3)

    def across(step):
        return pltpu.make_async_remote_copy(
            src_ref=strip_map,
            dst_ref=maps.at[strip],
            send_sem=map_send.at[step],
            recv_sem=map_recv.at[strip],
            device_id=device_at(row, lax.rem(col + step, cols) * pairs + pair),
            device_id_type=MESH,
        )

    def onward(source, column, step):
        slot = column * pairs + pair
        return pltpu.make_async_remote_copy(
            src_ref=source,
            dst_ref=maps.at[slot],
            send_sem=on_send.at[column * pairs + step],
            recv_sem=map_recv.at[slot],
            device_id=device_at(row, col * pairs + lax.rem(pair + step, pairs)),
            device_id_type=MESH,
        )

    def arrival(slot):
        return pltpu.make_async_remote_copy(
            src_ref=strip_map,
            dst_ref=maps.at[slot],
            send_sem=map_send.at[0],
            recv_sem=map_recv.at[slot],
            device_id=device_at(row, strip),
            device_id_type=MESH,
        )

    for step in range(1, cols):
        across(step).start()
    finish = post(rows, me, row_device, lambda peer: blocks.at[peer], landing, send_sem, recv_sem)
    for step in range(1, pairs):
        onward(strip_map, col, step).start()
    landing[me] = blocks[me]
    maps[strip] = strip_map[...]
    for step in range(1, cols):
        column = lax.rem(col + step, cols)
        slot = column * pairs + pair
        arrival(slot).wait_recv()
        for other in range(1, pairs):
            onward(maps.at[slot], column, other).start()
    finish()
    out[...] = total_of(rows, landing).astype(out.dtype)
    for step in range(1, cols):
        across(step).wait_send()
    for step in range(cols):
        column = lax.rem(col + step, cols)
        for other in range(1, pairs):
            onward(strip_map, column, other).wait_send()
            arrival(column * pairs + lax.rem(pair + other, pairs)).wait_recv()


def reduce_scatter(blocks, strip_map, number):
    rows, strips = group_size("rows"), group_size("strips")
    return pl.pallas_call(
        scatter_kernel,
        out_shape=(
            jax.ShapeDtypeStruct(blocks.shape[1:], jnp.bfloat16),
            jax.ShapeDtypeStruct((strips,) + strip_map.shape, strip_map.dtype),
        ),
        in_specs=[VMEM] * 2,
        out_specs=(VMEM,) * 2,
        scratch_shapes=[pltpu.VMEM(blocks.shape, blocks.dtype)]
        + sems(rows)
        + sems(strips)
        + [pltpu.SemaphoreType.DMA((strips,))],
        compiler_params=params(number),
    )(blocks, strip_map)


def last_kernel(
    scale, shifted, gradient, maps, whole, out, taps, turned, blocks, landing, part, parts, mine, *semaphores
):
    rows, row, row_device = group("rows")
    strips, strip, strip_device = group("strips")
    barrier = pltpu.get_barrier_semaphore()
    for step in range(1, rows):
        pl.semaphore_signal(
            barrier, inc=1, device_id=row_device(lax.rem(row + step, rows)), device_id_type=MESH
        )
    for step in range(1, strips):
        pl.semaphore_signal(
            barrier, inc=1, device_id=strip_device(lax.rem(strip + step, strips)), device_id_type=MESH
        )
    band, channels, width = gradient.shape
    steps, filters, spots = turned.shape
    full2 = whole.shape[1] - 2
    chunk = spots // full2
    quads = whole.shape[2]

    def one_row(h, total):
        patches = shifted[pl.ds(h + 1, 3), :, pl.ds(width, width)].reshape(9 * channels, width)
        return total + lax.dot_general(
            gradient[h], patches, (((1,), (1,)), ((), ())), preferred_element_type=jnp.float32
        )

    total = lax.fori_loop(0, band, one_row, jnp.zeros((channels, 9 * channels), jnp.float32))
    height = channels // strips
    for peer in range(strips):
        blocks[peer] = total[peer * height : (peer + 1) * height].astype(blocks.dtype)

    for step in range(steps):
        rows_of = maps[pl.ds(step * chunk, chunk), :, pl.ds(quads, filters)].reshape(spots, filters)
        turned[step] = rows_of.astype(jnp.float32).T.astype(turned.dtype)

    def tap(index):
        first, second = divmod(index, 3)

        def product(step):
            window = whole[pl.ds(step * chunk + first, chunk), pl.ds(second, full2)]
            return scale * jnp.dot(
                turned[step], window.reshape(spots, quads), preferred_element_type=jnp.float32
            )

        taps[index] = product(0)
        if steps > 1:
            @pl.loop(1, steps)
            def _(step):
                taps[index] += product(step)

    pl.semaphore_wait(barrier, rows + strips - 2)
    one, two, three = semaphores[:2], semaphores[2:4], semaphores[4:]
    finish = post(strips, strip, strip_device, lambda peer: blocks.at[peer], landing, *one)
    landing[strip] = blocks[strip]
    for index in range(3):
        tap(index)
    finish()
    total = total_of(strips, landing).astype(part.dtype)
    part[...] = total
    finish = post(rows, row, row_device, lambda peer: part, parts, *two)
    parts[row] = total
    for index in range(3, 6):
        tap(index)
    finish()
    total = total_of(rows, parts).astype(part.dtype)
    mine[...] = total
    finish = post(strips, strip, strip_device, lambda peer: mine, out, *three)
    out[strip] = total
    for index in range(6, 9):
        tap(index)
    finish()


def last_layer(shifted, gradient, maps, whole, scale, number):
    rows, strips = group_size("rows"), group_size("strips")
    channels = gradient.shape[1]
    kind = jnp.bfloat16
    height2, full2, depth = maps.shape
    filters = depth - whole.shape[2]
    chunk = max(1, 1024 // full2)
    piece = (channels // strips, 9 * channels)
    return pl.pallas_call(
        functools.partial(last_kernel, scale),
        out_shape=(
            jax.ShapeDtypeStruct((strips,) + piece, kind),
            jax.ShapeDtypeStruct((9, filters, whole.shape[2]), jnp.float32),
        ),
        in_specs=[VMEM] * 4,
        out_specs=(VMEM,) * 2,
        scratch_shapes=[
            pltpu.VMEM((height2 // chunk, filters, chunk * full2), kind),
            pltpu.VMEM((strips,) + piece, kind),
            pltpu.VMEM((strips,) + piece, kind),
            pltpu.VMEM(piece, kind),
            pltpu.VMEM((rows,) + piece, kind),
            pltpu.VMEM(piece, kind),
        ]
        + sems(strips)
        + sems(rows)
        + sems(strips),
        compiler_params=params(number),
    )(shifted, gradient, maps, whole)


def conv_valid(cells, kernel, numbers):
    return lax.conv_general_dilated(
        cells[None], kernel, (1, 1), "VALID", dimension_numbers=numbers, preferred_element_type=jnp.float32
    )[0]


def flip_kernel(kernel):
    return jnp.transpose(kernel[:, ::-1, ::-1, :], (3, 1, 2, 0))


def silu_slope(values):
    sigmoid_value = jax.nn.sigmoid(values)
    return sigmoid_value * (1.0 + values * (1.0 - sigmoid_value))


def local(features_in, filters_one, filters_two, out_grad):
    channels, band, width = features_in.shape
    rows, strips = lax.axis_size("row"), lax.axis_size(STRIP)
    row, strip = place()
    quads = channels * 4
    band2, width2 = band // 4, width // 4
    height2, full2 = band2 * rows, width2 * strips
    filters = filters_two.shape[0]

    shifted, pre_one, own, upstream = first_layer(
        features_in, jnp.transpose(out_grad, (2, 1, 0)), filters_one, 0
    )
    pre_two = conv_valid(
        jnp.pad(own, ((1, 1), (0, 0), (0, 0))), filters_two, ("NHWC", "OHWI", "NHWC")
    )
    near = (upstream.astype(jnp.float32) * silu_slope(pre_two)).astype(jnp.bfloat16)

    spread = conv_valid(
        jnp.pad(near, ((1, 1), (0, 0), (0, 0))), flip_kernel(filters_two), ("NHWC", "OHWI", "NHWC")
    )
    channel = jnp.arange(quads)
    low_row = (channel // 2) % 2 == 1
    low_col = channel % 2 == 1
    tall = jnp.pad(spread, ((1, 1), (0, 0), (0, 0)))
    bands = spread.reshape(rows, band2, width2 + 2, quads)
    rim = jnp.where(low_row, tall[0:height2:band2], tall[band2 + 1 : height2 + 2 : band2])
    bands = jnp.concatenate([bands, rim[:, None]], 1)
    edge = jnp.where(low_col, bands[:, :, :1], bands[:, :, -1:])
    bands = jnp.concatenate([bands[:, :, 1:-1], edge], 2).astype(jnp.bfloat16)
    spots = (band2 + 1) * (width2 + 1)
    bands = jnp.pad(bands.reshape(rows, spots, quads), ((0, 0), (0, -spots % 16), (0, 0)))
    strip_map = jnp.concatenate([own[:, 3:-3], near[:, 2:-2]], 2).reshape(height2 * width2, quads + filters)
    grad_pooled, maps = reduce_scatter(bands, strip_map, 2)

    by_part = jnp.arange(quads)
    order = 4 * (by_part % channels) + by_part // channels
    pick = (channel[:, None] == order[None]).astype(jnp.bfloat16)
    parts = jnp.dot(grad_pooled[:spots], pick, preferred_element_type=jnp.float32).astype(jnp.bfloat16)
    parts = parts.reshape(band2 + 1, width2 + 1, 2, 2, channels)
    source = (jnp.arange(width + 2) + 1) // 2
    source = jnp.where(source == 0, 2 * width2 + 1, source - 1)
    place_of = 2 * jnp.arange(width2 + 1)[:, None] + jnp.arange(2)[None]
    expand = (place_of[:, :, None] == source[None, None]).astype(jnp.bfloat16)
    halves = jnp.einsum("uvijc,vjw->uicw", parts, expand, preferred_element_type=jnp.float32)
    halves = halves.reshape(2 * band2 + 2, channels, width + 2)
    halves = jnp.concatenate([halves[-1:], halves[:-1]], 0)
    tall_grad = jnp.repeat(halves, 2, 0)[1:-1] * 0.25
    at_row = row * band - 1 + jnp.arange(band + 2)
    at_col = strip * width - 1 + jnp.arange(width + 2)
    inside = ((at_row >= 0) & (at_row < band * rows))[:, None, None] & (
        (at_col >= 0) & (at_col < width * strips)
    )
    grad_ext = jnp.where(inside, tall_grad * silu_slope(pre_one), 0.0).astype(jnp.bfloat16)

    maps = jnp.transpose(maps.reshape(strips, height2, width2, quads + filters), (1, 0, 2, 3))
    maps = maps.reshape(height2, full2, quads + filters)
    whole = jnp.pad(maps[:, :, :quads], ((1, 1), (1, 1), (0, 0)))
    summed, taps = last_layer(
        shifted,
        grad_ext[1:-1, :, 1:-1],
        maps,
        whole,
        1.0 / math.sqrt(height2 * full2),
        3,
    )
    grad_ext, summed = lax.optimization_barrier((grad_ext, summed))
    scale = 1.0 / math.sqrt(band * rows * width * strips)
    grad_one = summed.astype(jnp.float32).reshape(channels, 3, 3, channels) * scale
    grad_two = jnp.transpose(taps, (1, 0, 2)).reshape(filters, 3, 3, quads)

    input_grad = conv_valid(
        jnp.transpose(grad_ext, (1, 0, 2)), flip_kernel(filters_one), ("NCHW", "OHWI", "NCHW")
    ).astype(jnp.bfloat16)

    return (input_grad, grad_one, grad_two)


def solution(mesh):
    in_specs = (
        P("grp", "row", ("col", "pair")),
        P(),
        P("row", None, None, None),
        P(("grp", "row"), ("col", "pair"), None),
    )
    out_specs = (
        P("grp", "row", ("col", "pair")),
        P("grp", None, None, None),
        P(("grp", "row"), None, None, None),
    )
    return jax.shard_map(local, mesh=mesh, in_specs=in_specs, out_specs=out_specs, check_vma=False)
```

profile of v0, /device:TPU:0, one launch (start us, length us, event | category | flops | bytes accessed | tf_op | source)
XLA Modules:
  0.0 56.9 jit_solution(3630584930057949752)
XLA Ops:
  1.1 0.7 %broadcast_and_fusion = pred[10,130]{1,0:T(8,128)(4,1)} fusion(pred[130]{0:T(512)(128)(4,1)S(1)} %compare_and_fusion.1, pred[10]{0:T(512)(128)(4,1)S(1)} %compare_and_fusion.2), kind=kLoop, calls=%fused_computation.65 | loop fusion | flops 1300 | bytes 1440 | tf_op jit(solution)/shard_map/and | solution.py:570
  1.9 0.9 %copy.74 = bf16[128,32,8]{0,1,2:T(8,128)(2,1)S(1)} copy(bf16[128,32,8]{0,2,1:T(8,128)(2,1)} %param.7) | data formatting | bytes 131072 | tf_op args[3]
  2.9 0.9 %copy.73 = bf16[64,8,128]{2,0,1:T(8,128)(2,1)S(1)} copy(bf16[64,8,128]{2,1,0:T(8,128)(2,1)} %param.4) | data formatting | bytes 262144 | tf_op args[0]
  3.8 1.0 %copy.39 = bf16[64,3,3,64]{0,3,2,1:T(8,128)(2,1)S(1)} copy(bf16[64,3,3,64]{3,0,2,1:T(8,128)(2,1)} %param.5) | data formatting | bytes 147456 | tf_op args[1]
  4.9 0.1 copy.40.kernel
  5.0 18.1 %shard_map.67 = (bf16[2,16,128]{2,1,0:T(8,128)(2,1)S(1)}, f32[10,64,384]{2,1,0:T(8,128)S(1)}, bf16[4,80,256]{2,1,0:T(8,128)(2,1)S(1)}, bf16[12,192,384]{2,1,0:T(8,128)(2,1)S(1)}) custom-call(bf16[8,64,128]{2,1,0:T(8,128)(2,1)S(1)} %bitcast.90, bf16[2,16,128]{2,1,0:T(8,128)(2,1)S(1)} %pad_maximum_fusion.4.edge_up, bf16[64,576]{1,0:T(8,128)(2,1)S(1)} %copy.40.kernel, ...), custom_call_target="tpu_custom_call" | custom-call | tf_op jit(solution)/shard_map/pallas_call | solution.py:203
  23.2 1.2 %fusion.13 = f32[1,8,36,128]{3,0,2,1:T(1,128)S(1)} fusion(bf16[128,3,3,256]{3,0,2,1:T(8,128)(2,1)S(1)} %copy-done, bf16[1,10,38,256]{3,2,1,0:T(8,128)(2,1)S(1)} %pad_bitcast_fusion), kind=kOutput, calls=%fused_computation.22 | convolution fusion | flops 169869312 | bytes 931840 | tf_op jit(solution)/shard_map/conv_general_dilated | solution.py:507
  24.6 1.0 %fusion.17 = bf16[1,8,34,256]{3,0,2,1:T(2,128)(2,1)S(1)} fusion(bf16[128,3,3,256]{3,0,2,1:T(8,128)(2,1)S(1)} %copy-done, bf16[1,10,36,128]{3,2,1,0:T(8,128)(2,1)S(1)} %pad_bitcast_fusion.1), kind=kOutput, calls=%fused_computation.33 | convolution fusion | flops 160432128 | bytes 821248 | tf_op jit(solution)/shard_map/conv_general_dilated | solution.py:507
  25.7 0.1 copy.61
  25.9 0.4 slice.67
  26.3 0.4 slice.66
  26.9 0.3 fusion.6
  27.2 0.2 pad_maximum_fusion.1
  27.5 8.7 %shard_map.68 = (bf16[112,256]{1,0:T(8,128)(2,1)S(1)}, bf16[4,256,384]{2,1,0:T(8,128)(2,1)S(1)}) custom-call(bf16[4,112,256]{2,1,0:T(8,128)(2,1)S(1)} %pad.23.blocks, bf16[256,384]{1,0:T(8,128)(2,1)S(1)} %bitcast.87), custom_call_target="tpu_custom_call" | custom-call | tf_op jit(solution)/shard_map/pallas_call | solution.py:386
  36.2 0.2 convolution_convert_fusion
  36.4 0.1 copy.51
  36.5 0.2 reshape.270
  36.7 0.3 convolution_bitcast_fusion
  37.2 1.0 %copy-done.4 = f32[10,64,384]{2,1,0:T(8,128)S(1)} copy-done((f32[10,64,384]{2,1,0:T(8,128)S(1)}, f32[10,64,384]{2,1,0:T(8,128)}, u32[]{:S(2)}) %copy-start.4) | copy-done | bytes 983064
  38.2 0.3 fusion.4
  38.6 0.1 slice.94.gradient
  38.7 0.1 pad.24.whole
  38.9 12.3 %shard_map.69 = (bf16[4,16,576]{2,1,0:T(8,128)(2,1)S(1)}, f32[9,128,256]{2,1,0:T(8,128)S(1)}) custom-call(bf16[12,192,384]{2,1,0:T(8,128)(2,1)S(1)} %get-tuple-element.17.shifted, bf16[8,64,128]{2,1,0:T(8,128)(2,1)S(1)} %slice.94.gradient, bf16[8,128,384]{2,1,0:T(8,128)(2,1)S(1)} %bitcast.84, bf16[10,130,256]{2,1,0:T(8,128)(2,1)S(1)} %pad.24.whole), custom_call_target="tpu_custom_call" | custom-call | tf_op jit(solution)/shard_map/pallas_call | solution.py:483
  51.2 1.0 %copy-done.1 = f32[9,128,256]{2,1,0:T(8,128)} copy-done((f32[9,128,256]{2,1,0:T(8,128)}, f32[9,128,256]{2,1,0:T(8,128)S(1)}, u32[]{:S(2)}) %copy-start.1) | copy-done | bytes 1179672
  52.2 0.3 copy.63
  52.5 0.1 reshape.277
  52.8 0.6 %copy-done.5 = bf16[64,3,3,64]{3,0,2,1:T(8,128)(2,1)S(1)} copy-done((bf16[64,3,3,64]{3,0,2,1:T(8,128)(2,1)S(1)}, bf16[64,3,3,64]{3,0,2,1:T(8,128)(2,1)}, u32[]{:S(2)}) %copy-start.5) | copy-done | bytes 73752
  53.4 0.6 %fusion = bf16[8,8,17,64]{3,1,2,0:T(8,128)(2,1)S(1)} fusion(bf16[64,3,3,64]{3,0,2,1:T(8,128)(2,1)S(1)} %copy-done.5, bf16[64,10,1,7,2]{0,3,4,1,2:T(8,128)(2,1)S(1)} %slice.96, bf16[64,10,1,8,17]{0,3,4,1,2:T(8,128)(2,1)S(1)} %copy.54, pred[8,17]{0,1:T(8,128)(4,1)S(1)} %copy-done.7), kind=kOutput, calls=%fused_computation.1 | convolution fusion | flops 80939008 | bytes 405128 | tf_op jit(solution)/shard_map/conv_general_dilated | solution.py:507
  54.0 0.9 %copy.56 = bf16[64,8,128]{2,1,0:T(8,128)(2,1)} copy(bf16[64,8,128]{0,1,2:T(8,128)(2,1)S(1)} %slice_bitcast_fusion) | data formatting | bytes 262144
  54.9 0.2 mul.120
  55.1 0.7 %copy.57 = f32[64,3,3,64]{3,0,2,1:T(8,128)} copy(f32[64,3,3,64]{3,2,1,0:T(4,128)S(1)} %mul.120) | data formatting | bytes 294912
  55.8 1.0 %copy.76 = f32[128,3,3,256]{3,0,2,1:T(8,128)} copy(f32[128,3,3,256]{3,0,2,1:T(8,128)S(1)} %bitcast.85) | data formatting | bytes 2359296
  (65 shorter events, 1.7 us)
Async XLA Ops:
  0.6 22.6 %copy-start = (bf16[128,3,3,256]{3,0,2,1:T(8,128)(2,1)S(1)}, bf16[128,3,3,256]{3,0,2,1:T(8,128)(2,1)}, u32[]{:S(2)}) copy-start(bf16[128,3,3,256]{3,0,2,1:T(8,128)(2,1)} %param.6) | copy-start | bytes 1769476
  23.1 1.3 %copy-start.3 = (f32[10,64,384]{2,1,0:T(8,128)}, f32[10,64,384]{2,1,0:T(8,128)S(1)}, u32[]{:S(2)}) copy-start(f32[10,64,384]{2,1,0:T(8,128)S(1)} %get-tuple-element.16) | copy-start | bytes 2949124
  37.0 1.2 %copy-start.4 = (f32[10,64,384]{2,1,0:T(8,128)S(1)}, f32[10,64,384]{2,1,0:T(8,128)}, u32[]{:S(2)}) copy-start(f32[10,64,384]{2,1,0:T(8,128)} %copy-done.3) | copy-start | bytes 2949124
  37.0 1.2 %copy-start.6 = (pred[10,130]{1,0:T(8,128)(4,1)S(1)}, pred[10,130]{1,0:T(8,128)(4,1)}, u32[]{:S(2)}) copy-start(pred[10,130]{1,0:T(8,128)(4,1)} %broadcast_and_fusion) | copy-start | bytes 3904
  51.2 1.0 %copy-start.1 = (f32[9,128,256]{2,1,0:T(8,128)}, f32[9,128,256]{2,1,0:T(8,128)S(1)}, u32[]{:S(2)}) copy-start(f32[9,128,256]{2,1,0:T(8,128)S(1)} %get-tuple-element.22) | copy-start | bytes 3538948
  52.4 0.9 %copy-start.5 = (bf16[64,3,3,64]{3,0,2,1:T(8,128)(2,1)S(1)}, bf16[64,3,3,64]{3,0,2,1:T(8,128)(2,1)}, u32[]{:S(2)}) copy-start(bf16[64,3,3,64]{3,0,2,1:T(8,128)(2,1)} %param.5) | copy-start | bytes 221188
  52.5 0.9 %copy-start.7 = (pred[8,17]{0,1:T(8,128)(4,1)S(1)}, pred[8,17]{0,1:T(8,128)(4,1)}, u32[]{:S(2)}) copy-start(pred[8,17]{0,1:T(8,128)(4,1)} %constant.140) | copy-start | bytes 412
  54.0 1.8 %copy-start.2 = (f32[9,128,256]{2,1,0:T(8,128)S(1)}, f32[9,128,256]{2,1,0:T(8,128)}, u32[]{:S(2)}) copy-start(f32[9,128,256]{2,1,0:T(8,128)} %copy-done.1) | copy-start | bytes 3538948
where the time goes:
time: 57.1 us; the launch traced here: 56.9 us
  Pallas kernels  39.1 us (68%)
  local copies, waits for them, and re-layouts  11.4 us (20%)
  matrix products  3.16 us (6%)
  other arithmetic  2 us (4%)
  between operations  1.17 us (2%)
    pallas_call x1, Pallas kernels, first_layer(): pl.pallas_call(functools.partial(first_kernel, rows, strips), out_shape=(...  18.1 us
    pallas_call x1, Pallas kernels, last_layer(): pl.pallas_call(functools.partial(last_kernel, scale), out_shape=(jax.Shap...  12.3 us
    pallas_call x1, Pallas kernels, reduce_scatter(): pl.pallas_call(scatter_kernel, out_shape=(jax.ShapeDtypeStruct(blocks.sha...  8.7 us
    unnamed x24, local copies, waits for them, and re-layouts  8.42 us
    conv_general_dilated x3, matrix products, conv_valid(): lax.conv_general_dilated(cells[None], kernel, (1, 1), 'VALID', dimension_...  2.73 us

commit v1 on v0

v1 whole, which is shorter than its diff:
```python
import functools
import math

import jax
import jax.numpy as jnp
from jax import lax
from jax.experimental import pallas as pl
from jax.experimental.pallas import tpu as pltpu
from jax.sharding import PartitionSpec as P

MESH = pl.DeviceIdType.MESH
VMEM = pl.BlockSpec(memory_space=pltpu.VMEM)
ANY = pl.BlockSpec(memory_space=pl.ANY)
STRIP = ("col", "pair")
BF = jnp.bfloat16
F32 = jnp.float32

EDGE = 4

DIAGONALS = [(a, b) for a in (-1, 1) for b in (-1, 1)]
WAYS = [(0, -1), (0, 1), (-1, 0), (1, 0)] + DIAGONALS

BY_LANES = (((1,), (1,)), ((), ()))
BY_ROWS = (((0,), (0,)), ((), ()))


def place():
    return lax.axis_index("row"), lax.axis_index(STRIP)


def device_at(row, strip):
    pairs = lax.axis_size("pair")
    return (lax.axis_index("grp"), row, lax.div(strip, pairs), lax.rem(strip, pairs))


def sems(count):
    return [pltpu.SemaphoreType.DMA((count,)), pltpu.SemaphoreType.DMA((count,))]


def post(count, me, device_of, source, landing, send_sem, recv_sem):
    def copy_of(step, slot):
        peer = lax.rem(me + step, count)
        return pltpu.make_async_remote_copy(
            src_ref=source(peer),
            dst_ref=landing.at[me if slot is None else slot],
            send_sem=send_sem.at[step],
            recv_sem=recv_sem.at[me if slot is None else slot],
            device_id=device_of(peer),
            device_id_type=MESH,
        )

    @pl.loop(1, count)
    def _(step):
        copy_of(step, None).start()

    def finish():
        @pl.loop(1, count)
        def _(step):
            copy_of(step, None).wait_send()
            copy_of(step, lax.rem(me + step, count)).wait_recv()

    return finish


def iota(shape, dim):
    return lax.broadcasted_iota(jnp.int32, shape, dim)


def dot(a, b, numbers=(((1,), (0,)), ((), ()))):
    return lax.dot_general(a, b, numbers, preferred_element_type=F32)


def slope(values):
    s = 1.0 / (1.0 + jnp.exp(-values))
    return s * (1.0 + values * (1.0 - s))


def total_of(count, landing):
    value = landing[0].astype(F32)
    for i in range(1, count):
        value += landing[i].astype(F32)
    return value


def whole_kernel(
    rows, strips, band, height2,
    x_any, f1_any, f2_any, up_any,
    ig_out, g1_out, g2_out,
    x_in, f1, f2, up_in, x_wide, x_turned, own, edges_f, edges, from_side, from_row, from_corner, from_up,
    tile, patches, w1, spread_one, pre, block, gathered, up_wide, up, pool3, near3, spread,
    blocks, landed, grad_f, grad, grad_own, pool_all, near_all, pool_map, near_map,
    mine_blocks, one_landed, one_part, one_parts, one_mine, one_all, g1_wide,
    load_sem, a_send, a_recv, b_send, b_recv, c_send, c_recv,
    d1_send, d1_recv, d2_send, d2_recv, d3_send, d3_recv,
    p_send, p_on, p_recv, n_send, n_on, n_recv,
):
    row, strip = place()
    cols, pairs = lax.axis_size("col"), lax.axis_size("pair")
    col, pair = lax.axis_index("col"), lax.axis_index("pair")
    channels = f1.shape[1]
    filters = f2.shape[1]
    quads = 4 * channels
    width = x_in.shape[1]
    width2 = width // 4
    band2 = band // 4
    span = width2 + 2 * EDGE
    full2 = width2 * strips
    mid = pl.ds(EDGE, width2)

    def row_device(i):
        return device_at(i, strip)

    def strip_device(i):
        return device_at(row, i)

    def there(way):
        a, b = row + way[0], strip + way[1]
        return (a >= 0) & (a < rows) & (b >= 0) & (b < strips)

    barrier = pltpu.get_barrier_semaphore()
    for step in range(1, rows):
        pl.semaphore_signal(barrier, inc=1, device_id=row_device(lax.rem(row + step, rows)), device_id_type=MESH)
    for step in range(1, strips):
        pl.semaphore_signal(
            barrier, inc=1, device_id=strip_device(lax.rem(strip + step, strips)), device_id_type=MESH
        )
    for way in DIAGONALS:
        @pl.when(there(way))
        def _(way=way):
            pl.semaphore_signal(
                barrier, inc=1, device_id=device_at(row + way[0], strip + way[1]), device_id_type=MESH
            )
    loads = [
        pltpu.make_async_copy(source, target, load_sem.at[n])
        for n, (source, target) in enumerate([(x_any, x_in), (up_any, up_in), (f1_any, f1), (f2_any, f2)])
    ]
    for load in loads:
        load.start()

    shape = (width, width)
    pick = (iota(shape, 1) == 4 * (iota(shape, 0) % width2) + iota(shape, 0) // width2).astype(BF)
    low_half = iota((width2, 128), 1) < channels
    loads[0].wait()
    x_wide[...] = x_in[...].astype(F32)
    for h in range(band):
        line = x_wide[pl.ds(h, channels, stride=band), :].astype(BF)
        x_turned[pl.ds(2 * h * channels, channels), :] = line
        x_turned[pl.ds((2 * h + 1) * channels, channels), :] = line
    turned = dot(pick, x_turned[...], BY_LANES)
    for h in range(band):
        lanes = slice(h * 128, (h + 1) * 128)
        for half in range(2):
            even = turned[2 * half * width2 : (2 * half + 1) * width2, lanes]
            odd = turned[(2 * half + 1) * width2 : (2 * half + 2) * width2, lanes]
            value = jnp.where(low_half, even, odd)
            tile[h + 2, mid, pl.ds(half * 128, 128)] = value
            own[pl.ds(h * width2, width2), pl.ds(half * 128, 128)] = value.astype(BF)
    for h in range(band):
        edges_f[0, pl.ds(h * EDGE, EDGE)] = tile[h + 2, pl.ds(EDGE, EDGE)]
        edges_f[1, pl.ds(h * EDGE, EDGE)] = tile[h + 2, pl.ds(width2, EDGE)]
    edges[...] = edges_f[:, : band * EDGE].astype(BF)
    loads[1].wait()

    diagonals = (jnp.where(row > 0, 1, 0) + jnp.where(row < rows - 1, 1, 0)) * (
        jnp.where(strip > 0, 1, 0) + jnp.where(strip < strips - 1, 1, 0)
    )
    pl.semaphore_wait(barrier, rows - 1 + strips - 1 + diagonals)
    edge_rows = band * EDGE
    up_edge = 2 * height2

    def slot_of(way):
        side, top = (way[1] + 1) // 2, (way[0] + 1) // 2
        if way[0] == 0:
            return from_side.at[side]
        if way[1] == 0:
            return from_row.at[top]
        return from_corner.at[2 * top + side]

    def source_of(way):
        side = (way[1] + 1) // 2
        if way[0] == 0:
            return edges.at[side]
        if way[1] == 0:
            return own.at[pl.ds(0 if way[0] < 0 else (band - 2) * width2, 2 * width2)]
        return edges.at[side, pl.ds(0 if way[0] < 0 else edge_rows - 16, 16)]

    def border(way, arriving=False):
        back = (-way[0], -way[1])
        land = way if arriving else back
        return pltpu.make_async_remote_copy(
            src_ref=source_of(way),
            dst_ref=slot_of(land),
            send_sem=a_send.at[WAYS.index(way)],
            recv_sem=a_recv.at[WAYS.index(land)],
            device_id=device_at(row + way[0], strip + way[1]),
            device_id_type=MESH,
        )

    def up_border(side, arriving=False):
        land = side if arriving else 1 - side
        return pltpu.make_async_remote_copy(
            src_ref=up_in.at[pl.ds(0 if side == 0 else up_in.shape[0] - up_edge, up_edge)],
            dst_ref=from_up.at[land],
            send_sem=a_send.at[len(WAYS) + side],
            recv_sem=a_recv.at[len(WAYS) + land],
            device_id=device_at(row, strip + (-1, 1)[side]),
            device_id_type=MESH,
        )

    for way in WAYS:
        @pl.when(there(way))
        def _(way=way):
            border(way).start()

        @pl.when(jnp.logical_not(there(way)))
        def _(way=way):
            slot = slot_of(way)
            slot[...] = jnp.zeros(slot.shape, slot.dtype)

    for side in range(2):
        @pl.when(there((0, (-1, 1)[side])))
        def _(side=side):
            up_border(side).start()

        @pl.when(jnp.logical_not(there((0, (-1, 1)[side]))))
        def _(side=side):
            from_up[side] = jnp.zeros(from_up.shape[1:], BF)

    loads[2].wait()
    zero = jnp.zeros((channels, channels), F32)
    nothing = jnp.zeros((channels, 128), BF)
    for i in range(3):
        a, b, c = [f1[3 * i + j].astype(F32) for j in range(3)]
        bc, ab, za, cz = [
            jnp.concatenate(two, 1).astype(BF) for two in ((b, c), (a, b), (zero, a), (c, zero))
        ]
        table = (
            (bc, nothing, za, nothing),
            (ab, cz, nothing, nothing),
            (za, bc, nothing, nothing),
            (nothing, ab, nothing, cz),
        )
        for p in range(4):
            for k in range(4):
                w1[pl.ds(p * channels, channels), pl.ds(i * 512 + k * 128, 128)] = table[p][k]
    shape = (quads, quads)
    for i in range(2):
        target = 4 * (iota(shape, 0) % channels) + 2 * i + iota(shape, 0) // (2 * channels)
        spread_one[pl.ds(i * quads, quads)] = (iota(shape, 1) == target).astype(BF)

    for way in WAYS:
        @pl.when(there(way))
        def _(way=way):
            border(way, True).wait_recv()
    for side in range(2):
        edge = from_side[side].astype(F32)
        at = pl.ds(0 if side == 0 else EDGE + width2, EDGE)
        for h in range(band):
            tile[h + 2, at] = edge[h * EDGE : (h + 1) * EDGE]
        beyond = from_row[side].astype(F32)
        for h in range(2):
            tile[h if side == 0 else band + 2 + h, mid] = beyond[h * width2 : (h + 1) * width2]
        for top in range(2):
            corner = from_corner[2 * top + side].astype(F32)
            for h in range(2):
                start = 16 - 2 * EDGE + h * EDGE if top == 0 else h * EDGE
                tile[h if top == 0 else band + 2 + h, at] = corner[start : start + EDGE]
    for h in range(band + 4):
        here = tile[h]
        patches[h, :, pl.ds(0, quads)] = here.astype(BF)
        patches[h, :, pl.ds(quads, 128)] = pltpu.roll(here[:, quads - 128 :], 1, 0).astype(BF)
        patches[h, :, pl.ds(quads + 128, 128)] = pltpu.roll(here[:, :128], span - 1, 0).astype(BF)

    lines = band + 2
    windows = jnp.concatenate([patches[i : i + lines].reshape(lines * span, 512) for i in range(3)], 1)
    pre[0:lines] = dot(windows, w1[...], BY_LANES).reshape(lines, span, quads)

    def silu(values):
        return values / (1.0 + jnp.exp(-values))

    terms = []
    for i in range(2):
        total = []
        for u in range(band2):
            at = 1 + 4 * u + 2 * i
            total.append((silu(pre[at]) + silu(pre[at + 1])) * 0.25)
        total = jnp.concatenate(total, 0)
        upper = total.astype(BF)
        terms.append((upper, (total - upper.astype(F32)).astype(BF)))
    pooled = jnp.zeros((band2 * span, quads), F32)
    for i in range(2):
        for term in terms[i]:
            pooled += dot(term, spread_one[pl.ds(i * quads, quads)])
    at_col = strip * width2 - EDGE + iota((band2 * span, quads), 0) % span
    pooled = jnp.where((at_col >= 0) & (at_col < full2), pooled, 0.0).astype(BF)
    block[...] = pooled
    finish = post(rows, row, row_device, lambda peer: block, gathered, b_send, b_recv)
    gathered[row] = pooled

    for h in range(lines):
        pre[h] = slope(pre[h]) * 0.25
    for side in range(2):
        @pl.when(there((0, (-1, 1)[side])))
        def _(side=side):
            up_border(side, True).wait_recv()
    up_wide[pl.ds(0, up_edge)] = from_up[0].astype(F32)
    up_wide[pl.ds(up_edge, width2 * height2)] = up_in[...].astype(F32)
    up_wide[pl.ds(up_edge + width2 * height2, up_edge)] = from_up[1].astype(F32)
    for u in range(height2):
        up[u, pl.ds(0, 2)] = jnp.zeros((2, filters), F32)
        up[u, pl.ds(2, width2 + 4)] = up_wide[pl.ds(u, width2 + 4, stride=height2), :]
        up[u, pl.ds(width2 + 6, 2)] = jnp.zeros((2, filters), F32)
    pool3[0] = jnp.zeros(pool3.shape[1:], BF)
    pool3[height2 + 1] = jnp.zeros(pool3.shape[1:], BF)
    for j in range(3):
        near3[j, 0] = jnp.zeros(near3.shape[2:], BF)
        near3[j, height2 + 1] = jnp.zeros(near3.shape[2:], BF)
    spread[0] = jnp.zeros(spread.shape[1:], F32)
    spread[height2 + 1] = jnp.zeros(spread.shape[1:], F32)
    loads[3].wait()
    finish()

    def across(source, table, send_sem, recv_sem, step):
        return pltpu.make_async_remote_copy(
            src_ref=source,
            dst_ref=table.at[strip],
            send_sem=send_sem.at[step],
            recv_sem=recv_sem.at[strip],
            device_id=device_at(row, lax.rem(col + step, cols) * pairs + pair),
            device_id_type=MESH,
        )

    def onward(table, send_sem, recv_sem, column, step):
        slot = column * pairs + pair
        return pltpu.make_async_remote_copy(
            src_ref=table.at[slot],
            dst_ref=table.at[slot],
            send_sem=send_sem.at[column * pairs + step],
            recv_sem=recv_sem.at[slot],
            device_id=device_at(row, col * pairs + lax.rem(pair + step, pairs)),
            device_id_type=MESH,
        )

    def arrival(table, send_sem, recv_sem, slot):
        return pltpu.make_async_remote_copy(
            src_ref=table.at[slot],
            dst_ref=table.at[slot],
            send_sem=send_sem.at[0],
            recv_sem=recv_sem.at[slot],
            device_id=device_at(row, lax.rem(col + 1, cols) * pairs + pair),
            device_id_type=MESH,
        )

    def share(table, send_sem, on_sem, recv_sem):
        for step in range(1, cols):
            across(table.at[strip], table, send_sem, recv_sem, step).start()
        for step in range(1, pairs):
            onward(table, on_sem, recv_sem, col, step).start()

    def pass_on(table, send_sem, on_sem, recv_sem):
        for step in range(1, cols):
            column = lax.rem(col + step, cols)
            arrival(table, send_sem, recv_sem, column * pairs + pair).wait_recv()
            for other in range(1, pairs):
                onward(table, on_sem, recv_sem, column, other).start()

    def settle(table, send_sem, on_sem, recv_sem):
        for step in range(1, cols):
            across(table.at[strip], table, send_sem, recv_sem, step).wait_send()
        for step in range(cols):
            column = lax.rem(col + step, cols)
            for other in range(1, pairs):
                onward(table, on_sem, recv_sem, column, other).wait_send()
                slot = column * pairs + lax.rem(pair + other, pairs)
                arrival(table, send_sem, recv_sem, slot).wait_recv()

    for u in range(height2):
        r, k = divmod(u, band2)
        here = gathered[r, pl.ds(k * span, span)]
        wide = here.astype(F32)
        pool3[u + 1, :, pl.ds(0, quads)] = pltpu.roll(wide, 1, 0).astype(BF)
        pool3[u + 1, :, pl.ds(quads, quads)] = here
        pool3[u + 1, :, pl.ds(2 * quads, quads)] = pltpu.roll(wide, span - 1, 0).astype(BF)
        pool_all[strip, pl.ds(u * width2, width2)] = wide[EDGE : EDGE + width2].astype(BF)
    pool_sems = (p_send, p_on, p_recv)
    share(pool_all, *pool_sems)
    spots = height2 * span
    windows = jnp.concatenate([pool3[i : i + height2].reshape(spots, 3 * quads) for i in range(3)], 1)
    kernel = jnp.concatenate([f2[t] for t in range(9)], 1)
    pre_two = dot(windows, kernel, BY_LANES)
    near = up[0:height2].reshape(spots, filters) * slope(pre_two)
    near3[0, 1 : height2 + 1] = pltpu.roll(near, spots - 1, 0).astype(BF).reshape(height2, span, filters)
    near3[1, 1 : height2 + 1] = near.astype(BF).reshape(height2, span, filters)
    near3[2, 1 : height2 + 1] = pltpu.roll(near, 1, 0).astype(BF).reshape(height2, span, filters)
    total = jnp.zeros((spots, quads), F32)
    if filters % 128 == 0:
        windows = [near3[j, 2 - i : 2 - i + height2].reshape(spots, filters) for i in range(3) for j in range(3)]
        total = dot(jnp.concatenate(windows, 1), f2[...].reshape(9 * filters, quads))
    else:
        for t in range(9):
            i, j = divmod(t, 3)
            total += dot(near3[j, 2 - i : 2 - i + height2].reshape(spots, filters), f2[t])
    spread[1 : height2 + 1] = total.reshape(height2, span, quads)

    lane = iota((1, quads), 1)
    low_row = (lane // 2) % 2 == 1
    low_col = lane % 2 == 1
    at_row = iota((16, quads), 0)

    def fill(peer):
        top = peer * band2
        cells = [spread[top + 1 + k] for k in range(band2)]
        cells.append(jnp.where(low_row, spread[top], spread[top + band2 + 1]))
        tail = jnp.zeros((16, quads), F32)
        for k, cell in enumerate(cells):
            blocks[peer, pl.ds(k * width2, width2)] = cell[EDGE : EDGE + width2].astype(BF)
            rim = jnp.where(low_col, cell[EDGE - 1 : EDGE], cell[EDGE + width2 : EDGE + width2 + 1])
            tail = jnp.where(at_row == k, rim, tail)
        blocks[peer, pl.ds((band2 + 1) * width2, 16)] = tail.astype(BF)

    for peer in range(rows):
        fill(peer)
    finish = post(rows, row, row_device, lambda peer: blocks.at[peer], landed, c_send, c_recv)
    landed[row] = blocks[row]
    for u in range(height2):
        near_all[strip, pl.ds(u * width2, width2)] = near[
            u * span + EDGE : u * span + EDGE + width2
        ].astype(BF)
    near_sems = (n_send, n_on, n_recv)
    share(near_all, *near_sems)
    pass_on(pool_all, *pool_sems)
    finish()
    parts = total_of(rows, landed).astype(BF)
    parts = dot(parts, spread_one[...], BY_LANES)

    for line in range(lines):
        h = line - 1
        if h < 0:
            k, i, inside = band2, 1, row > 0
        elif h >= band:
            k, i, inside = band2, 0, row < rows - 1
        else:
            k, i, inside = h // 4, (h // 2) % 2, None
        some = parts[:, i * quads : (i + 1) * quads]
        body = some[k * width2 : (k + 1) * width2] * pre[line, mid]
        rim = some[(band2 + 1) * width2 + k : (band2 + 1) * width2 + k + 1]
        left = jnp.where(strip > 0, rim * pre[line, pl.ds(EDGE - 1, 1)], 0.0)
        right = jnp.where(strip < strips - 1, rim * pre[line, pl.ds(EDGE + width2, 1)], 0.0)
        if inside is not None:
            body, left, right = [jnp.where(inside, value, 0.0) for value in (body, left, right)]
        else:
            grad_f[h, pl.ds(0, EDGE)] = jnp.zeros((EDGE, quads), F32)
            grad_f[h, mid] = body
            grad_f[h, pl.ds(EDGE + width2, EDGE)] = jnp.zeros((EDGE, quads), F32)
            grad_own[h] = grad_f[h].astype(BF)
        at = min(max(h, 0), band - 1)
        if inside is not None:
            at = band
            grad_f[at, pl.ds(0, EDGE)] = jnp.zeros((EDGE, quads), F32)
            grad_f[at, mid] = body
            grad_f[at, pl.ds(EDGE + width2, EDGE)] = jnp.zeros((EDGE, quads), F32)
        grad_f[at, pl.ds(EDGE - 1, 1)] = left
        grad_f[at, pl.ds(EDGE + width2, 1)] = right
        grad[line] = grad_f[at].astype(BF)

    low = iota((channels, 128), 1) < channels
    halves, ends = [], []
    own_spots = band * span
    windows = jnp.concatenate([patches[1 + i : 1 + i + band].reshape(own_spots, 512) for i in range(3)], 1)
    taps = dot(grad_own[...].reshape(own_spots, quads), windows, BY_ROWS)

    def cut(i, p, k):
        return taps[p * channels : (p + 1) * channels, i * 512 + k * 128 : i * 512 + (k + 1) * 128]

    for i in range(3):
        bc = pltpu.roll(cut(i, 0, 0) + cut(i, 2, 1), 64, 1)
        ab = cut(i, 1, 0) + cut(i, 3, 1)
        za = pltpu.roll(cut(i, 0, 2) + cut(i, 2, 0), 64, 1)
        cz = cut(i, 1, 1) + cut(i, 3, 3)
        halves.append(ab + jnp.where(low, za, bc))
        ends.append(cz + bc)
    packed = halves + [jnp.where(low, ends[0], pltpu.roll(ends[1], 64, 1)), jnp.where(low, ends[2], 0.0)]
    packed = jnp.concatenate(packed, 0).astype(BF)
    piece = mine_blocks.shape[1]
    for s in range(strips):
        start, stop = s * piece, min((s + 1) * piece, packed.shape[0])
        if stop > start:
            mine_blocks[s, pl.ds(0, stop - start)] = packed[start:stop]
        if stop - start < piece:
            begin = max(stop - start, 0)
            mine_blocks[s, pl.ds(begin, piece - begin)] = jnp.zeros((piece - begin, 128), BF)
    finish = post(strips, strip, strip_device, lambda peer: mine_blocks.at[peer], one_landed, d1_send, d1_recv)
    one_landed[strip] = mine_blocks[strip]

    pass_on(near_all, *near_sems)
    cells = jnp.concatenate([grad[2 - i : 2 - i + band].reshape(own_spots, quads) for i in range(3)], 1)
    kernel = jnp.concatenate([w1[:, i * 512 : (i + 1) * 512] for i in range(3)], 0)
    total = dot(cells, kernel)
    before = pltpu.roll(total[:, quads : quads + 128], own_spots - 1, 0)
    after = pltpu.roll(total[:, quads + 128 :], 1, 0)
    sides = (total[:, :128] + after, total[:, 128:quads] + before)
    turned = []
    for h in range(band):
        lines_of = []
        for b in range(4):
            value = sides[b // 2][h * span + EDGE : h * span + EDGE + width2]
            lines_of.append(jnp.where(low_half == (b % 2 == 0), value, 0.0).astype(BF))
        turned.append(jnp.concatenate(lines_of, 0))
    turned = dot(jnp.concatenate(turned, 1), pick, BY_ROWS)
    for h in range(band):
        at = 2 * h * channels
        x_wide[pl.ds(h, channels, stride=band), :] = (
            turned[at : at + channels] + turned[at + channels : at + 2 * channels]
        )
    ig_out[...] = x_wide[...].astype(BF)

    finish()
    part = total_of(strips, one_landed).astype(BF)
    one_part[...] = part
    finish = post(rows, row, row_device, lambda peer: one_part, one_parts, d2_send, d2_recv)
    one_parts[row] = part

    settle(pool_all, *pool_sems)
    settle(near_all, *near_sems)
    near_map[0] = jnp.zeros(near_map.shape[1:], BF)
    near_map[height2 + 1] = jnp.zeros(near_map.shape[1:], BF)
    at_lane = iota((filters, full2), 1)

    def assemble(u):
        at = u * width2
        if not isinstance(u, int):
            at = pl.multiple_of(at, width2)
        line = [near_all[s, pl.ds(at, width2)].astype(F32) for s in range(strips)]
        line = jnp.concatenate(line, 0).T
        after = jnp.where(at_lane < full2 - 1, pltpu.roll(line, full2 - 1, 1), 0.0)
        before = jnp.where(at_lane > 0, pltpu.roll(line, 1, 1), 0.0)
        for j, value in enumerate((after, line, before)):
            near_map[u + 1, pl.ds(j * filters, filters)] = value.astype(BF)
        for s in range(strips):
            pool_map[u, pl.ds(s * width2, width2)] = pool_all[s, pl.ds(at, width2)]

    chunk = max(1, 1024 // full2)
    steps = height2 // chunk
    if steps == 1:
        for u in range(height2):
            assemble(u)
    else:
        pl.loop(0, height2)(assemble)

    def filter_taps(i, step):
        at = step * chunk
        left = jnp.concatenate([near_map[at + k + 2 - i] for k in range(chunk)], 1)
        right = pool_map[pl.ds(at, chunk)].reshape(chunk * full2, quads)
        return dot(left, right).reshape(3, filters, quads)

    def filter_gradient(i):
        g2_out[3 * i : 3 * i + 3] = filter_taps(i, 0)
        if steps > 1:
            @pl.loop(1, steps)
            def _(step):
                g2_out[3 * i : 3 * i + 3] += filter_taps(i, step)

    filter_gradient(0)
    finish()
    part = total_of(rows, one_parts).astype(BF)
    one_mine[...] = part
    finish = post(strips, strip, strip_device, lambda peer: one_mine, one_all, d3_send, d3_recv)
    one_all[strip] = part
    filter_gradient(1)
    filter_gradient(2)
    for way in WAYS:
        @pl.when(there(way))
        def _(way=way):
            border(way).wait_send()
    for side in range(2):
        @pl.when(there((0, (-1, 1)[side])))
        def _(side=side):
            up_border(side).wait_send()
    finish()
    done = one_all[...].astype(F32).reshape(strips * piece, 128)
    rolled = pltpu.roll(done, 64, 1)
    for i in range(3):
        for j in range(3):
            k = i if j < 2 else 3 + i // 2
            value = done if (j if j < 2 else i % 2) == 0 else rolled
            g1_out[3 * i + j] = value[k * channels : (k + 1) * channels, :channels]


def local(features_in, filters_one, filters_two, out_grad):
    channels, band, width = features_in.shape
    rows, strips = lax.axis_size("row"), lax.axis_size(STRIP)
    cols, pairs = lax.axis_size("col"), lax.axis_size("pair")
    filters = filters_two.shape[0]
    quads = 4 * channels
    height2 = out_grad.shape[2]
    width2, band2 = width // 4, band // 4
    span = width2 + 2 * EDGE
    full2 = width2 * strips
    spots = (band2 + 1) * width2 + 16
    piece = -(-5 * channels // strips // 16) * 16

    def v(shape, kind=BF):
        return pltpu.VMEM(shape, kind)

    scratch = [
        v((channels * band, width)),
        v((9, channels, channels)),
        v((9, filters, quads)),
        v((width2 * height2, filters)),
        v((channels * band, width), F32),
        v((2 * channels * band, width)),
        v((band * width2, quads)),
        v((2, band * EDGE + 8, quads), F32),
        v((2, band * EDGE, quads)),
        v((2, band * EDGE, quads)),
        v((2, 2 * width2, quads)),
        v((4, 16, quads)),
        v((2, 2 * height2, filters)),
        v((band + 5, span, quads), F32),
        v((band + 4, span, 512)),
        v((quads, 3 * 512)),
        v((2 * quads, quads)),
        v((band + 3, span, quads), F32),
        v((band2 * span, quads)),
        v((rows, band2 * span, quads)),
        v((span * height2, filters), F32),
        v((height2 + 1, span, filters), F32),
        v((height2 + 2, span, 3 * quads)),
        v((3, height2 + 2, span, filters)),
        v((height2 + 2, span, quads), F32),
        v((rows, spots, quads)),
        v((rows, spots, quads)),
        v((band + 2, span, quads), F32),
        v((band + 2, span, quads)),
        v((band, span, quads)),
        v((strips, height2 * width2, quads)),
        v((strips, height2 * width2, filters)),
        v((height2, full2, quads)),
        v((height2 + 2, 3 * filters, full2)),
        v((strips, piece, 128)),
        v((strips, piece, 128)),
        v((piece, 128)),
        v((rows, piece, 128)),
        v((piece, 128)),
        v((strips, piece, 128)),
        v((8, 128)),
        pltpu.SemaphoreType.DMA((4,)),
    ]
    scratch += sems(len(WAYS) + 2) + sems(rows) + sems(rows) + sems(strips) + sems(rows) + sems(strips)
    for _ in range(2):
        scratch += [
            pltpu.SemaphoreType.DMA((cols,)),
            pltpu.SemaphoreType.DMA((cols * pairs,)),
            pltpu.SemaphoreType.DMA((strips,)),
        ]
    share = 1 if rows * strips <= 64 else 2
    ig, g1, g2 = pl.pallas_call(
        functools.partial(whole_kernel, rows, strips, band, height2),
        out_shape=(
            jax.ShapeDtypeStruct((channels * band, width), BF),
            jax.ShapeDtypeStruct((9, channels, channels), F32),
            jax.ShapeDtypeStruct((9, filters, quads), F32),
        ),
        in_specs=[ANY] * 4,
        out_specs=(VMEM,) * 3,
        scratch_shapes=scratch,
        compiler_params=pltpu.CompilerParams(
            collective_id=0, has_side_effects=True, vmem_limit_bytes=share * 28 * 1024 * 1024
        ),
    )(
        features_in.reshape(channels * band, width),
        jnp.transpose(filters_one, (1, 2, 0, 3)).reshape(9, channels, channels),
        jnp.transpose(filters_two, (1, 2, 0, 3)).reshape(9, filters, quads),
        jnp.transpose(out_grad, (1, 2, 0)).reshape(width2 * height2, filters),
    )
    scale_one = 1.0 / math.sqrt(band * rows * width * strips)
    scale_two = 1.0 / math.sqrt(height2 * full2)
    grad_one = jnp.transpose((g1 * scale_one).reshape(3, 3, channels, channels), (2, 0, 1, 3))
    grad_two = jnp.transpose((g2 * scale_two).reshape(3, 3, filters, quads), (2, 0, 1, 3))
    return (ig.reshape(channels, band, width), grad_one, grad_two)


def solution(mesh):
    in_specs = (
        P("grp", "row", ("col", "pair")),
        P(),
        P("row", None, None, None),
        P(("grp", "row"), ("col", "pair"), None),
    )
    out_specs = (
        P("grp", "row", ("col", "pair")),
        P("grp", None, None, None),
        P(("grp", "row"), None, None, None),
    )
    return jax.shard_map(local, mesh=mesh, in_specs=in_specs, out_specs=out_specs, check_vma=False)
```

time: 57.1 us -> 41.6 us (0.73)
  local copies, waits for them, and re-layouts: 11.4 us -> 4.36 us
  Pallas kernels: 39.1 us -> 34.5 us
  matrix products: 3.16 us -> 0 us
    pallas_call x3 -> x1, Pallas kernels: 39.1 us -> 34.5 us  [local(): pl.pallas_call(functools.partial(whole_kernel, rows, strips, band, height...]
    unnamed x24 -> x9, local copies, waits for them, and re-layouts: 8.42 us -> 4.36 us
    conv_general_dilated x3 -> x0, matrix products: 2.73 us -> none  [conv_valid(): lax.conv_general_dilated(cells[None], kernel, (1, 1), 'VALID', dimension_...]
    mul x4 -> x2, other arithmetic: 0.02 us -> 1.87 us  [the longest x1 1.13 us: local(): g2 * scale_two]
    slice x10 -> x0, local copies, waits for them, and re-layouts: 1.07 us -> none  [the longest x1 0.45 us: local(): tall[band2 + 1:height2 + 2:band2]]
    and x4 -> x0, other arithmetic: 0.69 us -> none  [the longest x1 0.67 us: local(): ((at_row >= 0) & (at_row < band * rows))[:, None, None]]
    convert_element_type x4 -> x0, other arithmetic: 0.65 us -> none  [the longest x1 0.35 us: local(): jnp.where(inside, tall_grad * silu_slope(pre_one), 0.0).astype(jnp.bfloat16)]
where the time goes in v1:
time: 41.6 us; the launch traced here: 41.4 us
  Pallas kernels  34.5 us (83%)
  local copies, waits for them, and re-layouts  4.36 us (10%)
  other arithmetic  1.87 us (4%)
  between operations  0.65 us (2%)
    pallas_call x1, Pallas kernels, local(): pl.pallas_call(functools.partial(whole_kernel, rows, strips, band, height...  34.5 us
    unnamed x9, local copies, waits for them, and re-layouts  4.36 us
    mul x1, other arithmetic, local(): g2 * scale_two  1.13 us

profile of v1, /device:TPU:0, one launch (start us, length us, event | category | flops | bytes accessed | tf_op | source)
XLA Modules:
  0.0 41.4 jit_solution(10763705539793137213)
XLA Ops:
  0.6 0.0 copy-start
  0.6 1.1 %copy-done = bf16[128,3,3,256]{3,0,2,1:T(8,128)(2,1)S(1)} copy-done((bf16[128,3,3,256]{3,0,2,1:T(8,128)(2,1)S(1)}, bf16[128,3,3,256]{3,0,2,1:T(8,128)(2,1)}, u32[]{:S(2)}) %copy-start) | copy-done | bytes 589848
  1.7 0.0 copy-start.1
  1.7 0.9 %copy-done.1 = bf16[64,3,3,64]{3,0,2,1:T(8,128)(2,1)S(1)} copy-done((bf16[64,3,3,64]{3,0,2,1:T(8,128)(2,1)S(1)}, bf16[64,3,3,64]{3,0,2,1:T(8,128)(2,1)}, u32[]{:S(2)}) %copy-start.1) | copy-done | bytes 73752
  2.6 0.0 copy-start.2
  2.6 0.9 %copy-done.2 = bf16[64,8,128]{2,1,0:T(8,128)(2,1)S(1)} copy-done((bf16[64,8,128]{2,1,0:T(8,128)(2,1)S(1)}, bf16[64,8,128]{2,1,0:T(8,128)(2,1)}, u32[]{:S(2)}) %copy-start.2) | copy-done | bytes 131096
  3.5 0.0 copy-start.3
  3.5 0.8 %copy-done.3 = bf16[128,32,8]{0,2,1:T(8,128)(2,1)S(1)} copy-done((bf16[128,32,8]{0,2,1:T(8,128)(2,1)S(1)}, bf16[128,32,8]{0,2,1:T(8,128)(2,1)}, u32[]{:S(2)}) %copy-start.3) | copy-done | bytes 65560
  4.4 34.5 %shard_map.67 = (bf16[512,128]{1,0:T(8,128)(2,1)S(1)}, f32[9,64,64]{2,1,0:T(8,128)S(1)}, f32[9,128,256]{2,1,0:T(8,128)S(1)}) custom-call(bf16[512,128]{1,0:T(8,128)(2,1)S(1)} %bitcast.19, bf16[9,64,64]{2,1,0:T(8,128)(2,1)S(1)} %bitcast.18, bf16[9,128,256]{2,1,0:T(8,128)(2,1)S(1)} %bitcast.17, bf16[256,128]{1,0:T(8,128)(2,1)S(1)} %bitcast.21), custom_call_target="tpu_custom_call" | custom-call | tf_op jit(solution)/shard_map/pallas_call | solution.py:657
  38.9 0.7 %broadcast_multiply_fusion.1 = f32[9,64,64]{2,1,0:T(8,128)} fusion(f32[9,64,64]{2,1,0:T(8,128)S(1)} %get-tuple-element.7), kind=kLoop, calls=%fused_computation.1 | loop fusion | flops 36864 | bytes 294912 | tf_op jit(solution)/shard_map/mul | solution.py:678
  39.6 1.1 %broadcast_multiply_fusion = f32[9,128,256]{2,1,0:T(8,128)} fusion(f32[9,128,256]{2,1,0:T(8,128)S(1)} %get-tuple-element.8), kind=kLoop, calls=%fused_computation | loop fusion | flops 294912 | bytes 2359296 | tf_op jit(solution)/shard_map/mul | solution.py:679
  40.7 0.7 %copy.8 = bf16[64,8,128]{2,1,0:T(8,128)(2,1)} copy(bf16[64,8,128]{2,1,0:T(8,128)(2,1)S(1)} %bitcast.20) | data formatting | bytes 262144
Async XLA Ops:
  0.6 1.1 %copy-start = (bf16[128,3,3,256]{3,0,2,1:T(8,128)(2,1)S(1)}, bf16[128,3,3,256]{3,0,2,1:T(8,128)(2,1)}, u32[]{:S(2)}) copy-start(bf16[128,3,3,256]{3,0,2,1:T(8,128)(2,1)} %param.6) | copy-start | bytes 1769476
  1.7 0.9 %copy-start.1 = (bf16[64,3,3,64]{3,0,2,1:T(8,128)(2,1)S(1)}, bf16[64,3,3,64]{3,0,2,1:T(8,128)(2,1)}, u32[]{:S(2)}) copy-start(bf16[64,3,3,64]{3,0,2,1:T(8,128)(2,1)} %param.5) | copy-start | bytes 221188
  2.6 0.9 %copy-start.2 = (bf16[64,8,128]{2,1,0:T(8,128)(2,1)S(1)}, bf16[64,8,128]{2,1,0:T(8,128)(2,1)}, u32[]{:S(2)}) copy-start(bf16[64,8,128]{2,1,0:T(8,128)(2,1)} %param.4) | copy-start | bytes 393220
  3.5 0.8 %copy-start.3 = (bf16[128,32,8]{0,2,1:T(8,128)(2,1)S(1)}, bf16[128,32,8]{0,2,1:T(8,128)(2,1)}, u32[]{:S(2)}) copy-start(bf16[128,32,8]{0,2,1:T(8,128)(2,1)} %param.7) | copy-start | bytes 196612

commit v2 on v1

--- a/solution.py
+++ b/solution.py
@@ -10,7 +10,7 @@
 
 MESH = pl.DeviceIdType.MESH
 VMEM = pl.BlockSpec(memory_space=pltpu.VMEM)
-ANY = pl.BlockSpec(memory_space=pl.ANY)
+HBM = pl.BlockSpec(memory_space=pltpu.HBM)
 STRIP = ("col", "pair")
 BF = jnp.bfloat16
 F32 = jnp.float32
@@ -83,7 +83,7 @@
 
 
 def whole_kernel(
-    rows, strips, band, height2,
+    rows, strips, band, height2, scale_one, scale_two,
     x_any, f1_any, f2_any, up_any,
     ig_out, g1_out, g2_out,
     x_in, f1, f2, up_in, x_wide, x_turned, own, edges_f, edges, from_side, from_row, from_corner, from_up,
@@ -551,7 +551,7 @@
         at = step * chunk
         left = jnp.concatenate([near_map[at + k + 2 - i] for k in range(chunk)], 1)
         right = pool_map[pl.ds(at, chunk)].reshape(chunk * full2, quads)
-        return dot(left, right).reshape(3, filters, quads)
+        return scale_two * dot(left, right).reshape(3, filters, quads)
 
     def filter_gradient(i):
         g2_out[3 * i : 3 * i + 3] = filter_taps(i, 0)
@@ -577,13 +577,34 @@
         def _(side=side):
             up_border(side).wait_send()
     finish()
-    done = one_all[...].astype(F32).reshape(strips * piece, 128)
+    done = scale_one * one_all[...].astype(F32).reshape(strips * piece, 128)
     rolled = pltpu.roll(done, 64, 1)
     for i in range(3):
         for j in range(3):
             k = i if j < 2 else 3 + i // 2
             value = done if (j if j < 2 else i % 2) == 0 else rolled
             g1_out[3 * i + j] = value[k * channels : (k + 1) * channels, :channels]
+
+
+def write_kernel(*refs):
+    count = len(refs) // 2
+    sources, targets, sem = refs[:count], refs[count:-1], refs[-1]
+    copies = [pltpu.make_async_copy(sources[n], targets[n], sem.at[n]) for n in range(count)]
+    for copy in copies:
+        copy.start()
+    for copy in copies:
+        copy.wait()
+
+
+def write_out(*arrays):
+    arrays = [pltpu.with_memory_space_constraint(a, pltpu.VMEM) for a in arrays]
+    return pl.pallas_call(
+        write_kernel,
+        out_shape=tuple(jax.ShapeDtypeStruct(a.shape, a.dtype) for a in arrays),
+        in_specs=[VMEM] * len(arrays),
+        out_specs=(HBM,) * len(arrays),
+        scratch_shapes=[pltpu.SemaphoreType.DMA((len(arrays),))],
+    )(*arrays)
 
 
 def local(features_in, filters_one, filters_two, out_grad):
@@ -653,30 +674,33 @@
             pltpu.SemaphoreType.DMA((cols * pairs,)),
             pltpu.SemaphoreType.DMA((strips,)),
         ]
+    arguments = (
+        features_in.reshape(channels * band, width),
+        jnp.transpose(filters_one, (1, 2, 0, 3)).reshape(9, channels, channels),
+        jnp.transpose(filters_two, (1, 2, 0, 3)).reshape(9, filters, quads),
+        jnp.transpose(out_grad, (1, 2, 0)).reshape(width2 * height2, filters),
+    )
+    arguments = [pltpu.with_memory_space_constraint(a, pltpu.HBM) for a in arguments]
     share = 1 if rows * strips <= 64 else 2
+    scale_one = 1.0 / math.sqrt(band * rows * width * strips)
+    scale_two = 1.0 / math.sqrt(height2 * full2)
     ig, g1, g2 = pl.pallas_call(
-        functools.partial(whole_kernel, rows, strips, band, height2),
+        functools.partial(whole_kernel, rows, strips, band, height2, scale_one, scale_two),
         out_shape=(
             jax.ShapeDtypeStruct((channels * band, width), BF),
             jax.ShapeDtypeStruct((9, channels, channels), F32),
             jax.ShapeDtypeStruct((9, filters, quads), F32),
         ),
-        in_specs=[ANY] * 4,
+        in_specs=[HBM] * 4,
         out_specs=(VMEM,) * 3,
         scratch_shapes=scratch,
         compiler_params=pltpu.CompilerParams(
             collective_id=0, has_side_effects=True, vmem_limit_bytes=share * 28 * 1024 * 1024
         ),
-    )(
-        features_in.reshape(channels * band, width),
-        jnp.transpose(filters_one, (1, 2, 0, 3)).reshape(9, channels, channels),
-        jnp.transpose(filters_two, (1, 2, 0, 3)).reshape(9, filters, quads),
-        jnp.transpose(out_grad, (1, 2, 0)).reshape(width2 * height2, filters),
-    )
-    scale_one = 1.0 / math.sqrt(band * rows * width * strips)
-    scale_two = 1.0 / math.sqrt(height2 * full2)
-    grad_one = jnp.transpose((g1 * scale_one).reshape(3, 3, channels, channels), (2, 0, 1, 3))
-    grad_two = jnp.transpose((g2 * scale_two).reshape(3, 3, filters, quads), (2, 0, 1, 3))
+    )(*arguments)
+    ig, g1, g2 = write_out(ig, g1, g2)
+    grad_one = jnp.transpose(g1.reshape(3, 3, channels, channels), (2, 0, 1, 3))
+    grad_two = jnp.transpose(g2.reshape(3, 3, filters, quads), (2, 0, 1, 3))
     return (ig.reshape(channels, band, width), grad_one, grad_two)
 
 

time: 41.6 us -> 36.6 us (0.88)
  local copies, waits for them, and re-layouts: 4.36 us -> 0 us
  other arithmetic: 1.87 us -> 0 us
  Pallas kernels: 34.5 us -> 35.8 us
    unnamed x9 -> x0, local copies, waits for them, and re-layouts: 4.36 us -> none
    mul x2 -> x0, other arithmetic: 1.87 us -> none  [the longest x1 1.13 us: local(): g2 * scale_two]
    pallas_call x0 -> x1, Pallas kernels: none -> 1.18 us  [write_out(): pl.pallas_call(write_kernel, out_shape=tuple((jax.ShapeDtypeStruct(a.shap...]
where the time goes in v2:
time: 36.6 us; the launch traced here: 36.5 us
  Pallas kernels  35.8 us (98%)
  between operations  0.64 us (2%)
    pallas_call x1, Pallas kernels, local(): pl.pallas_call(functools.partial(whole_kernel, rows, strips, band, height...  34.6 us
    pallas_call x1, Pallas kernels, write_out(): pl.pallas_call(write_kernel, out_shape=tuple((jax.ShapeDtypeStruct(a.shap...  1.18 us

profile of v2, /device:TPU:0, one launch (start us, length us, event | category | flops | bytes accessed | tf_op | source)
XLA Modules:
  0.0 36.5 jit_solution(12129371128520169568)
XLA Ops:
  0.6 34.6 %shard_map.67 = (bf16[512,128]{1,0:T(8,128)(2,1)S(1)}, f32[9,64,64]{2,1,0:T(8,128)S(1)}, f32[9,128,256]{2,1,0:T(8,128)S(1)}) custom-call(bf16[512,128]{1,0:T(8,128)(2,1)} %bitcast.19, bf16[9,64,64]{2,1,0:T(8,128)(2,1)} %bitcast.18, bf16[9,128,256]{2,1,0:T(8,128)(2,1)} %bitcast.17, bf16[256,128]{1,0:T(8,128)(2,1)} %bitcast.20), custom_call_target="tpu_custom_call" | custom-call | tf_op jit(solution)/shard_map/pallas_call | solution.py:687
  35.3 1.2 %shard_map.68 = (bf16[512,128]{1,0:T(8,128)(2,1)}, f32[9,64,64]{2,1,0:T(8,128)}, f32[9,128,256]{2,1,0:T(8,128)}) custom-call(bf16[512,128]{1,0:T(8,128)(2,1)S(1)} %get-tuple-element.9.refs_0_, f32[9,64,64]{2,1,0:T(8,128)S(1)} %get-tuple-element.10.refs_1_, f32[9,128,256]{2,1,0:T(8,128)S(1)} %get-tuple-element.11.refs_2_), custom_call_target="tpu_custom_call" | custom-call | tf_op jit(solution)/shard_map/pallas_call | solution.py:601

commit v3 on v2

--- a/solution.py
+++ b/solution.py
@@ -37,27 +37,42 @@
     return [pltpu.SemaphoreType.DMA((count,)), pltpu.SemaphoreType.DMA((count,))]
 
 
-def post(count, me, device_of, source, landing, send_sem, recv_sem):
+def around(count, me):
+    return lambda step: lax.rem(me + step, count)
+
+
+def far_first(count, me):
+    def peer(step):
+        up = step - 1
+        up += jnp.where(up >= me, 1, 0)
+        down = count - step
+        down -= jnp.where(down <= me, 1, 0)
+        return jnp.where(me < count // 2, down, up)
+
+    return peer
+
+
+def post(count, me, order, device_of, source, landing, send_sem, recv_sem):
     def copy_of(step, slot):
-        peer = lax.rem(me + step, count)
+        peer = order(step)
         return pltpu.make_async_remote_copy(
             src_ref=source(peer),
-            dst_ref=landing.at[me if slot is None else slot],
+            dst_ref=landing.at[slot(peer)],
             send_sem=send_sem.at[step],
-            recv_sem=recv_sem.at[me if slot is None else slot],
+            recv_sem=recv_sem.at[slot(peer)],
             device_id=device_of(peer),
             device_id_type=MESH,
         )
 
     @pl.loop(1, count)
     def _(step):
-        copy_of(step, None).start()
+        copy_of(step, lambda peer: me).start()
 
     def finish():
         @pl.loop(1, count)
         def _(step):
-            copy_of(step, None).wait_send()
-            copy_of(step, lax.rem(me + step, count)).wait_recv()
+            copy_of(step, lambda peer: me).wait_send()
+            copy_of(step, lambda peer: peer).wait_recv()
 
     return finish
 
@@ -87,10 +102,10 @@
     x_any, f1_any, f2_any, up_any,
     ig_out, g1_out, g2_out,
     x_in, f1, f2, up_in, x_wide, x_turned, own, edges_f, edges, from_side, from_row, from_corner, from_up,
-    tile, patches, w1, spread_one, pre, block, gathered, up_wide, up, pool3, near3, spread,
-    blocks, landed, grad_f, grad, grad_own, pool_all, near_all, pool_map, near_map,
+    tile, patches, w1, spread_one, pre, block_f, block, gathered, up_wide, up, pool_f, pool3, near3, spread,
+    blocks, landed, grad_f, grad, grad_own, rims_f, rims, rim_rows, rim_side, rim_row, rim_corner, pool_all, near_all, pool_map, near_map,
     mine_blocks, one_landed, one_part, one_parts, one_mine, one_all, g1_wide,
-    load_sem, a_send, a_recv, b_send, b_recv, c_send, c_recv,
+    load_sem, a_send, a_recv, e_send, e_recv, b_send, b_recv, c_send, c_recv,
     d1_send, d1_recv, d2_send, d2_recv, d3_send, d3_recv,
     p_send, p_on, p_recv, n_send, n_on, n_recv,
 ):
@@ -106,6 +121,7 @@
     span = width2 + 2 * EDGE
     full2 = width2 * strips
     mid = pl.ds(EDGE, width2)
+    reach = width2 + 4
 
     def row_device(i):
         return device_at(i, strip)
@@ -153,11 +169,11 @@
             even = turned[2 * half * width2 : (2 * half + 1) * width2, lanes]
             odd = turned[(2 * half + 1) * width2 : (2 * half + 2) * width2, lanes]
             value = jnp.where(low_half, even, odd)
-            tile[h + 2, mid, pl.ds(half * 128, 128)] = value
+            tile[h + 1, mid, pl.ds(half * 128, 128)] = value
             own[pl.ds(h * width2, width2), pl.ds(half * 128, 128)] = value.astype(BF)
     for h in range(band):
-        edges_f[0, pl.ds(h * EDGE, EDGE)] = tile[h + 2, pl.ds(EDGE, EDGE)]
-        edges_f[1, pl.ds(h * EDGE, EDGE)] = tile[h + 2, pl.ds(width2, EDGE)]
+        edges_f[0, pl.ds(h * EDGE, EDGE)] = tile[h + 1, pl.ds(EDGE, EDGE)]
+        edges_f[1, pl.ds(h * EDGE, EDGE)] = tile[h + 1, pl.ds(width2, EDGE)]
     edges[...] = edges_f[:, : band * EDGE].astype(BF)
     loads[1].wait()
 
@@ -168,33 +184,67 @@
     edge_rows = band * EDGE
     up_edge = 2 * height2
 
-    def slot_of(way):
-        side, top = (way[1] + 1) // 2, (way[0] + 1) // 2
-        if way[0] == 0:
-            return from_side.at[side]
-        if way[1] == 0:
-            return from_row.at[top]
-        return from_corner.at[2 * top + side]
-
-    def source_of(way):
-        side = (way[1] + 1) // 2
-        if way[0] == 0:
-            return edges.at[side]
-        if way[1] == 0:
-            return own.at[pl.ds(0 if way[0] < 0 else (band - 2) * width2, 2 * width2)]
-        return edges.at[side, pl.ds(0 if way[0] < 0 else edge_rows - 16, 16)]
-
-    def border(way, arriving=False):
-        back = (-way[0], -way[1])
+    def corner_of(way):
+        return (way[1] + 1) // 2, (way[0] + 1) // 2
+
+    def border(kind, way, arriving=False):
+        (source_of, slot_of, send_sem, recv_sem), back = kind, (-way[0], -way[1])
         land = way if arriving else back
         return pltpu.make_async_remote_copy(
             src_ref=source_of(way),
             dst_ref=slot_of(land),
-            send_sem=a_send.at[WAYS.index(way)],
-            recv_sem=a_recv.at[WAYS.index(land)],
+            send_sem=send_sem.at[WAYS.index(way)],
+            recv_sem=recv_sem.at[WAYS.index(land)],
             device_id=device_at(row + way[0], strip + way[1]),
             device_id_type=MESH,
         )
+
+    def start_border(kind, way):
+        @pl.when(there(way))
+        def _():
+            border(kind, way).start()
+
+    def clear_border(kind, way):
+        @pl.when(jnp.logical_not(there(way)))
+        def _():
+            slot = kind[1](way)
+            slot[...] = jnp.zeros(slot.shape, slot.dtype)
+
+    def end_border(kind, way):
+        @pl.when(there(way))
+        def _():
+            border(kind, way, True).wait_recv()
+
+    def sent_border(kind, way):
+        @pl.when(there(way))
+        def _():
+            border(kind, way).wait_send()
+
+    def slots(side_slots, row_slots, corner_slots):
+        def slot_of(way):
+            side, top = corner_of(way)
+            if way[0] == 0:
+                return side_slots.at[side]
+            if way[1] == 0:
+                return row_slots.at[top]
+            return corner_slots.at[2 * top + side]
+
+        return slot_of
+
+    def cell_source(way):
+        side = corner_of(way)[0]
+        if way[0] == 0:
+            return edges.at[side]
+        if way[1] == 0:
+            return own.at[pl.ds(0 if way[0] < 0 else (band - 1) * width2, width2)]
+        return edges.at[side, pl.ds(0 if way[0] < 0 else edge_rows - 16, 16)]
+
+    def rim_source(way):
+        side, top = corner_of(way)
+        return rim_rows.at[top] if way[1] == 0 else rims.at[side]
+
+    cell_kind = (cell_source, slots(from_side, from_row, from_corner), a_send, a_recv)
+    rim_kind = (rim_source, slots(rim_side, rim_row, rim_corner), e_send, e_recv)
 
     def up_border(side, arriving=False):
         land = side if arriving else 1 - side
@@ -208,15 +258,10 @@
         )
 
     for way in WAYS:
-        @pl.when(there(way))
-        def _(way=way):
-            border(way).start()
-
-        @pl.when(jnp.logical_not(there(way)))
-        def _(way=way):
-            slot = slot_of(way)
-            slot[...] = jnp.zeros(slot.shape, slot.dtype)
-
+        start_border(cell_kind, way)
+    for way in WAYS:
+        clear_border(cell_kind, way)
+        clear_border(rim_kind, way)
     for side in range(2):
         @pl.when(there((0, (-1, 1)[side])))
         def _(side=side):
@@ -248,57 +293,71 @@
         target = 4 * (iota(shape, 0) % channels) + 2 * i + iota(shape, 0) // (2 * channels)
         spread_one[pl.ds(i * quads, quads)] = (iota(shape, 1) == target).astype(BF)
 
-    for way in WAYS:
-        @pl.when(there(way))
-        def _(way=way):
-            border(way, True).wait_recv()
+    def widen(line):
+        here = tile[line]
+        patches[line, :, pl.ds(0, quads)] = here.astype(BF)
+        patches[line, :, pl.ds(quads, 128)] = pltpu.roll(here[:, quads - 128 :], 1, 0).astype(BF)
+        patches[line, :, pl.ds(quads + 128, 128)] = pltpu.roll(here[:, :128], span - 1, 0).astype(BF)
+
+    def silu(values):
+        return values / (1.0 + jnp.exp(-values))
+
+    def pool(h):
+        total = (silu(pre[h]) + silu(pre[h + 1])) * 0.25
+        upper = total.astype(BF)
+        both = jnp.concatenate([upper, (total - upper.astype(F32)).astype(BF)], 0)
+        both = dot(both, spread_one[pl.ds((h // 2) % 2 * quads, quads)])
+        return both[:span] + both[span:]
+
+    side_at = [pl.ds(0, EDGE), pl.ds(EDGE + width2, EDGE)]
+    for way in WAYS[:2]:
+        end_border(cell_kind, way)
     for side in range(2):
         edge = from_side[side].astype(F32)
-        at = pl.ds(0 if side == 0 else EDGE + width2, EDGE)
         for h in range(band):
-            tile[h + 2, at] = edge[h * EDGE : (h + 1) * EDGE]
-        beyond = from_row[side].astype(F32)
-        for h in range(2):
-            tile[h if side == 0 else band + 2 + h, mid] = beyond[h * width2 : (h + 1) * width2]
-        for top in range(2):
+            tile[h + 1, side_at[side]] = edge[h * EDGE : (h + 1) * EDGE]
+    for line in range(1, band + 1):
+        widen(line)
+    windows = jnp.concatenate(
+        [patches[1 + i : band - 1 + i].reshape((band - 2) * span, 512) for i in range(3)], 1
+    )
+    pre[1 : band - 1] = dot(windows, w1[...], BY_LANES).reshape(band - 2, span, quads)
+    halves = {h: pool(h) for h in range(2, band - 2, 2)}
+
+    for way in WAYS[2:]:
+        end_border(cell_kind, way)
+    for top in range(2):
+        line = 0 if top == 0 else band + 1
+        tile[line, mid] = from_row[top].astype(F32)
+        for side in range(2):
             corner = from_corner[2 * top + side].astype(F32)
-            for h in range(2):
-                start = 16 - 2 * EDGE + h * EDGE if top == 0 else h * EDGE
-                tile[h if top == 0 else band + 2 + h, at] = corner[start : start + EDGE]
-    for h in range(band + 4):
-        here = tile[h]
-        patches[h, :, pl.ds(0, quads)] = here.astype(BF)
-        patches[h, :, pl.ds(quads, 128)] = pltpu.roll(here[:, quads - 128 :], 1, 0).astype(BF)
-        patches[h, :, pl.ds(quads + 128, 128)] = pltpu.roll(here[:, :128], span - 1, 0).astype(BF)
-
-    lines = band + 2
-    windows = jnp.concatenate([patches[i : i + lines].reshape(lines * span, 512) for i in range(3)], 1)
-    pre[0:lines] = dot(windows, w1[...], BY_LANES).reshape(lines, span, quads)
-
-    def silu(values):
-        return values / (1.0 + jnp.exp(-values))
-
-    terms = []
-    for i in range(2):
-        total = []
-        for u in range(band2):
-            at = 1 + 4 * u + 2 * i
-            total.append((silu(pre[at]) + silu(pre[at + 1])) * 0.25)
-        total = jnp.concatenate(total, 0)
-        upper = total.astype(BF)
-        terms.append((upper, (total - upper.astype(F32)).astype(BF)))
-    pooled = jnp.zeros((band2 * span, quads), F32)
-    for i in range(2):
-        for term in terms[i]:
-            pooled += dot(term, spread_one[pl.ds(i * quads, quads)])
+            tile[line, side_at[side]] = corner[16 - EDGE :] if top == 0 else corner[:EDGE]
+        widen(line)
+    windows = jnp.concatenate(
+        [jnp.concatenate([patches[i], patches[band - 1 + i]], 0) for i in range(3)], 1
+    )
+    ends = dot(windows, w1[...], BY_LANES)
+    pre[0] = ends[:span]
+    pre[band - 1] = ends[span:]
+    for h in (0, band - 2):
+        halves[h] = pool(h)
+    pooled = jnp.concatenate([halves[4 * u] + halves[4 * u + 2] for u in range(band2)], 0)
     at_col = strip * width2 - EDGE + iota((band2 * span, quads), 0) % span
-    pooled = jnp.where((at_col >= 0) & (at_col < full2), pooled, 0.0).astype(BF)
+    pooled = jnp.where((at_col >= 0) & (at_col < full2), pooled, 0.0)
+    for u in range(band2):
+        block_f[pl.ds(u * reach, reach)] = pooled[u * span + 2 : u * span + 2 + reach]
+    pooled = block_f[: band2 * reach].astype(BF)
     block[...] = pooled
-    finish = post(rows, row, row_device, lambda peer: block, gathered, b_send, b_recv)
+    finish = post(rows, row, far_first(rows, row), row_device, lambda peer: block, gathered, b_send, b_recv)
     gathered[row] = pooled
 
-    for h in range(lines):
+    for h in range(band):
         pre[h] = slope(pre[h]) * 0.25
+    grad_f[...] = jnp.zeros(grad_f.shape, F32)
+    rims_f[...] = jnp.zeros(rims_f.shape, F32)
+    for u in range(height2):
+        pool_f[u, pl.ds(0, 2)] = jnp.zeros((2, quads), F32)
+        pool_f[u, pl.ds(2 + reach, 2)] = jnp.zeros((2, quads), F32)
     for side in range(2):
         @pl.when(there((0, (-1, 1)[side])))
         def _(side=side):
@@ -315,8 +374,6 @@
     for j in range(3):
         near3[j, 0] = jnp.zeros(near3.shape[2:], BF)
         near3[j, height2 + 1] = jnp.zeros(near3.shape[2:], BF)
-    spread[0] = jnp.zeros(spread.shape[1:], F32)
-    spread[height2 + 1] = jnp.zeros(spread.shape[1:], F32)
     loads[3].wait()
     finish()
 
@@ -376,10 +433,10 @@
 
     for u in range(height2):
         r, k = divmod(u, band2)
-        here = gathered[r, pl.ds(k * span, span)]
-        wide = here.astype(F32)
+        pool_f[u, pl.ds(2, reach)] = gathered[r].astype(F32)[k * reach : (k + 1) * reach]
+        wide = pool_f[u]
         pool3[u + 1, :, pl.ds(0, quads)] = pltpu.roll(wide, 1, 0).astype(BF)
-        pool3[u + 1, :, pl.ds(quads, quads)] = here
+        pool3[u + 1, :, pl.ds(quads, quads)] = wide.astype(BF)
         pool3[u + 1, :, pl.ds(2 * quads, quads)] = pltpu.roll(wide, span - 1, 0).astype(BF)
         pool_all[strip, pl.ds(u * width2, width2)] = wide[EDGE : EDGE + width2].astype(BF)
     pool_sems = (p_send, p_on, p_recv)
@@ -400,27 +457,16 @@
         for t in range(9):
             i, j = divmod(t, 3)
             total += dot(near3[j, 2 - i : 2 - i + height2].reshape(spots, filters), f2[t])
-    spread[1 : height2 + 1] = total.reshape(height2, span, quads)
-
-    lane = iota((1, quads), 1)
-    low_row = (lane // 2) % 2 == 1
-    low_col = lane % 2 == 1
-    at_row = iota((16, quads), 0)
+    spread[...] = total.reshape(height2, span, quads)
 
     def fill(peer):
-        top = peer * band2
-        cells = [spread[top + 1 + k] for k in range(band2)]
-        cells.append(jnp.where(low_row, spread[top], spread[top + band2 + 1]))
-        tail = jnp.zeros((16, quads), F32)
-        for k, cell in enumerate(cells):
+        for k in range(band2):
+            cell = spread[peer * band2 + k]
             blocks[peer, pl.ds(k * width2, width2)] = cell[EDGE : EDGE + width2].astype(BF)
-            rim = jnp.where(low_col, cell[EDGE - 1 : EDGE], cell[EDGE + width2 : EDGE + width2 + 1])
-            tail = jnp.where(at_row == k, rim, tail)
-        blocks[peer, pl.ds((band2 + 1) * width2, 16)] = tail.astype(BF)
 
     for peer in range(rows):
         fill(peer)
-    finish = post(rows, row, row_device, lambda peer: blocks.at[peer], landed, c_send, c_recv)
+    finish = post(rows, row, far_first(rows, row), row_device, lambda peer: blocks.at[peer], landed, c_send, c_recv)
     landed[row] = blocks[row]
     for u in range(height2):
         near_all[strip, pl.ds(u * width2, width2)] = near[
@@ -433,40 +479,24 @@
     parts = total_of(rows, landed).astype(BF)
     parts = dot(parts, spread_one[...], BY_LANES)
 
-    for line in range(lines):
-        h = line - 1
-        if h < 0:
-            k, i, inside = band2, 1, row > 0
-        elif h >= band:
-            k, i, inside = band2, 0, row < rows - 1
-        else:
-            k, i, inside = h // 4, (h // 2) % 2, None
-        some = parts[:, i * quads : (i + 1) * quads]
-        body = some[k * width2 : (k + 1) * width2] * pre[line, mid]
-        rim = some[(band2 + 1) * width2 + k : (band2 + 1) * width2 + k + 1]
-        left = jnp.where(strip > 0, rim * pre[line, pl.ds(EDGE - 1, 1)], 0.0)
-        right = jnp.where(strip < strips - 1, rim * pre[line, pl.ds(EDGE + width2, 1)], 0.0)
-        if inside is not None:
-            body, left, right = [jnp.where(inside, value, 0.0) for value in (body, left, right)]
-        else:
-            grad_f[h, pl.ds(0, EDGE)] = jnp.zeros((EDGE, quads), F32)
-            grad_f[h, mid] = body
-            grad_f[h, pl.ds(EDGE + width2, EDGE)] = jnp.zeros((EDGE, quads), F32)
-            grad_own[h] = grad_f[h].astype(BF)
-        at = min(max(h, 0), band - 1)
-        if inside is not None:
-            at = band
-            grad_f[at, pl.ds(0, EDGE)] = jnp.zeros((EDGE, quads), F32)
-            grad_f[at, mid] = body
-            grad_f[at, pl.ds(EDGE + width2, EDGE)] = jnp.zeros((EDGE, quads), F32)
-        grad_f[at, pl.ds(EDGE - 1, 1)] = left
-        grad_f[at, pl.ds(EDGE + width2, 1)] = right
-        grad[line] = grad_f[at].astype(BF)
+    pass_on(near_all, *near_sems)
+    for h in range(band):
+        k, i = h // 4, (h // 2) % 2
+        body = parts[k * width2 : (k + 1) * width2, i * quads : (i + 1) * quads] * pre[h, mid]
+        grad_f[h + 1, mid] = body
+        grad_own[h] = grad_f[h + 1].astype(BF)
+        rims_f[0, pl.ds(h, 1)] = body[:1]
+        rims_f[1, pl.ds(h, 1)] = body[width2 - 1 :]
+        if h in (0, band - 1):
+            rim_rows[h // (band - 1)] = body.astype(BF)
+    rims[...] = rims_f[...].astype(BF)
+    for way in WAYS:
+        start_border(rim_kind, way)
 
     low = iota((channels, 128), 1) < channels
     halves, ends = [], []
     own_spots = band * span
-    windows = jnp.concatenate([patches[1 + i : 1 + i + band].reshape(own_spots, 512) for i in range(3)], 1)
+    windows = jnp.concatenate([patches[i : i + band].reshape(own_spots, 512) for i in range(3)], 1)
     taps = dot(grad_own[...].reshape(own_spots, quads), windows, BY_ROWS)
 
     def cut(i, p, k):
@@ -489,10 +519,68 @@
         if stop - start < piece:
             begin = max(stop - start, 0)
             mine_blocks[s, pl.ds(begin, piece - begin)] = jnp.zeros((piece - begin, 128), BF)
-    finish = post(strips, strip, strip_device, lambda peer: mine_blocks.at[peer], one_landed, d1_send, d1_recv)
+    finish = post(strips, strip, around(strips, strip), strip_device, lambda peer: mine_blocks.at[peer], one_landed, d1_send, d1_recv)
     one_landed[strip] = mine_blocks[strip]
 
-    pass_on(near_all, *near_sems)
+    settle(pool_all, *pool_sems)
+    settle(near_all, *near_sems)
+    near_map[0] = jnp.zeros(near_map.shape[1:], BF)
+    near_map[height2 + 1] = jnp.zeros(near_map.shape[1:], BF)
+    at_lane = iota((filters, full2), 1)
+
+    def assemble(u):
+        at = u * width2
+        if not isinstance(u, int):
+            at = pl.multiple_of(at, width2)
+        line = [near_all[s, pl.ds(at, width2)].astype(F32) for s in range(strips)]
+        line = jnp.concatenate(line, 0).T
+        after = jnp.where(at_lane < full2 - 1, pltpu.roll(line, full2 - 1, 1), 0.0)
+        before = jnp.where(at_lane > 0, pltpu.roll(line, 1, 1), 0.0)
+        for j, value in enumerate((after, line, before)):
+            near_map[u + 1, pl.ds(j * filters, filters)] = value.astype(BF)
+        for s in range(strips):
+            pool_map[u, pl.ds(s * width2, width2)] = pool_all[s, pl.ds(at, width2)]
+
+    chunk = max(1, 1024 // full2)
+    steps = height2 // chunk
+    if steps == 1:
+        for u in range(height2):
+            assemble(u)
+    else:
+        pl.loop(0, height2)(assemble)
+
+    def filter_taps(i, step):
+        at = step * chunk
+        left = jnp.concatenate([near_map[at + k + 2 - i] for k in range(chunk)], 1)
+        right = pool_map[pl.ds(at, chunk)].reshape(chunk * full2, quads)
+        return scale_two * dot(left, right).reshape(3, filters, quads)
+
+    def filter_gradient(i):
+        g2_out[3 * i : 3 * i + 3] = filter_taps(i, 0)
+        if steps > 1:
+            @pl.loop(1, steps)
+            def _(step):
+                g2_out[3 * i : 3 * i + 3] += filter_taps(i, step)
+
+    filter_gradient(0)
+
+    finish()
+    part = total_of(strips, one_landed).astype(BF)
+    one_part[...] = part
+    finish = post(rows, row, far_first(rows, row), row_device, lambda peer: one_part, one_parts, d2_send, d2_recv)
+    one_parts[row] = part
+
+    for way in WAYS:
+        end_border(rim_kind, way)
+    for h in range(band):
+        for side, at in ((0, EDGE - 1), (1, EDGE + width2)):
+            grad_f[h + 1, pl.ds(at, 1)] = rim_side[side].astype(F32)[h : h + 1]
+    for top, line, h in ((0, 0, band - 1), (1, band + 1, 0)):
+        grad_f[line, mid] = rim_row[top].astype(F32)
+        for side, at in ((0, EDGE - 1), (1, EDGE + width2)):
+            grad_f[line, pl.ds(at, 1)] = rim_corner[2 * top + side].astype(F32)[h : h + 1]
+    for line in range(band + 2):
+        grad[line] = grad_f[line].astype(BF)
     cells = jnp.concatenate([grad[2 - i : 2 - i + band].reshape(own_spots, quads) for i in range(3)], 1)
     kernel = jnp.concatenate([w1[:, i * 512 : (i + 1) * 512] for i in range(3)], 0)
     total = dot(cells, kernel)
@@ -514,64 +602,16 @@
         )
     ig_out[...] = x_wide[...].astype(BF)
 
-    finish()
-    part = total_of(strips, one_landed).astype(BF)
-    one_part[...] = part
-    finish = post(rows, row, row_device, lambda peer: one_part, one_parts, d2_send, d2_recv)
-    one_parts[row] = part
-
-    settle(pool_all, *pool_sems)
-    settle(near_all, *near_sems)
-    near_map[0] = jnp.zeros(near_map.shape[1:], BF)
-    near_map[height2 + 1] = jnp.zeros(near_map.shape[1:], BF)
-    at_lane = iota((filters, full2), 1)
-
-    def assemble(u):
-        at = u * width2
-        if not isinstance(u, int):
-            at = pl.multiple_of(at, width2)
-        line = [near_all[s, pl.ds(at, width2)].astype(F32) for s in range(strips)]
-        line = jnp.concatenate(line, 0).T
-        after = jnp.where(at_lane < full2 - 1, pltpu.roll(line, full2 - 1, 1), 0.0)
-        before = jnp.where(at_lane > 0, pltpu.roll(line, 1, 1), 0.0)
-        for j, value in enumerate((after, line, before)):
-            near_map[u + 1, pl.ds(j * filters, filters)] = value.astype(BF)
-        for s in range(strips):
-            pool_map[u, pl.ds(s * width2, width2)] = pool_all[s, pl.ds(at, width2)]
-
-    chunk = max(1, 1024 // full2)
-    steps = height2 // chunk
-    if steps == 1:
-        for u in range(height2):
-            assemble(u)
-    else:
-        pl.loop(0, height2)(assemble)
-
-    def filter_taps(i, step):
-        at = step * chunk
-        left = jnp.concatenate([near_map[at + k + 2 - i] for k in range(chunk)], 1)
-        right = pool_map[pl.ds(at, chunk)].reshape(chunk * full2, quads)
-        return scale_two * dot(left, right).reshape(3, filters, quads)
-
-    def filter_gradient(i):
-        g2_out[3 * i : 3 * i + 3] = filter_taps(i, 0)
-        if steps > 1:
-            @pl.loop(1, steps)
-            def _(step):
-                g2_out[3 * i : 3 * i + 3] += filter_taps(i, step)
-
-    filter_gradient(0)
+    filter_gradient(1)
     finish()
     part = total_of(rows, one_parts).astype(BF)
     one_mine[...] = part
-    finish = post(strips, strip, strip_device, lambda peer: one_mine, one_all, d3_send, d3_recv)
+    finish = post(strips, strip, around(strips, strip), strip_device, lambda peer: one_mine, one_all, d3_send, d3_recv)
     one_all[strip] = part
-    filter_gradient(1)
     filter_gradient(2)
     for way in WAYS:
-        @pl.when(there(way))
-        def _(way=way):
-            border(way).wait_send()
+        sent_border(cell_kind, way)
+        sent_border(rim_kind, way)
     for side in range(2):
         @pl.when(there((0, (-1, 1)[side])))
         def _(side=side):
@@ -617,7 +657,7 @@
     width2, band2 = width // 4, band // 4
     span = width2 + 2 * EDGE
     full2 = width2 * strips
-    spots = (band2 + 1) * width2 + 16
+    spots = band2 * width2
     piece = -(-5 * channels // strips // 16) * 16
 
     def v(shape, kind=BF):
@@ -634,26 +674,34 @@
         v((2, band * EDGE + 8, quads), F32),
         v((2, band * EDGE, quads)),
         v((2, band * EDGE, quads)),
-        v((2, 2 * width2, quads)),
+        v((2, width2, quads)),
         v((4, 16, quads)),
         v((2, 2 * height2, filters)),
-        v((band + 5, span, quads), F32),
-        v((band + 4, span, 512)),
+        v((band + 3, span, quads), F32),
+        v((band + 2, span, 512)),
         v((quads, 3 * 512)),
         v((2 * quads, quads)),
-        v((band + 3, span, quads), F32),
-        v((band2 * span, quads)),
-        v((rows, band2 * span, quads)),
+        v((band + 1, span, quads), F32),
+        v((band2 * (width2 + 4) + 8, quads), F32),
+        v((band2 * (width2 + 4), quads)),
+        v((rows, band2 * (width2 + 4), quads)),
         v((span * height2, filters), F32),
         v((height2 + 1, span, filters), F32),
+        v((height2 + 1, span, quads), F32),
         v((height2 + 2, span, 3 * quads)),
         v((3, height2 + 2, span, filters)),
-        v((height2 + 2, span, quads), F32),
+        v((height2, span, quads), F32),
         v((rows, spots, quads)),
         v((rows, spots, quads)),
-        v((band + 2, span, quads), F32),
+        v((band + 3, span, quads), F32),
         v((band + 2, span, quads)),
         v((band, span, quads)),
+        v((2, 16, quads), F32),
+        v((2, 16, quads)),
+        v((2, width2, quads)),
+        v((2, 16, quads)),
+        v((2, width2, quads)),
+        v((4, 16, quads)),
         v((strips, height2 * width2, quads)),
         v((strips, height2 * width2, filters)),
         v((height2, full2, quads)),
@@ -667,7 +715,7 @@
         v((8, 128)),
         pltpu.SemaphoreType.DMA((4,)),
     ]
-    scratch += sems(len(WAYS) + 2) + sems(rows) + sems(rows) + sems(strips) + sems(rows) + sems(strips)
+    scratch += sems(len(WAYS) + 2) + sems(len(WAYS)) + sems(rows) + sems(rows) + sems(strips) + sems(rows) + sems(strips)
     for _ in range(2):
         scratch += [
             pltpu.SemaphoreType.DMA((cols,)),

time: 36.6 us -> 33.9 us (0.926)
  Pallas kernels: 35.8 us -> 33.1 us
    pallas_call x1, Pallas kernels: 34.6 us -> 31.9 us  [local(): pl.pallas_call(functools.partial(whole_kernel, rows, strips, band, height...]
where the time goes in v3:
time: 33.9 us; the launch traced here: 33.7 us
  Pallas kernels  33.1 us (98%)
  between operations  0.64 us (2%)
    pallas_call x1, Pallas kernels, local(): pl.pallas_call(functools.partial(whole_kernel, rows, strips, band, height...  31.9 us
    pallas_call x1, Pallas kernels, write_out(): pl.pallas_call(write_kernel, out_shape=tuple((jax.ShapeDtypeStruct(a.shap...  1.18 us

profile of v3, /device:TPU:0, one launch (start us, length us, event | category | flops | bytes accessed | tf_op | source)
XLA Modules:
  0.0 33.7 jit_solution(10037307371138825538)
XLA Ops:
  0.6 31.9 %shard_map.67 = (bf16[512,128]{1,0:T(8,128)(2,1)S(1)}, f32[9,64,64]{2,1,0:T(8,128)S(1)}, f32[9,128,256]{2,1,0:T(8,128)S(1)}) custom-call(bf16[512,128]{1,0:T(8,128)(2,1)} %bitcast.19, bf16[9,64,64]{2,1,0:T(8,128)(2,1)} %bitcast.18, bf16[9,128,256]{2,1,0:T(8,128)(2,1)} %bitcast.17, bf16[256,128]{1,0:T(8,128)(2,1)} %bitcast.20), custom_call_target="tpu_custom_call" | custom-call | tf_op jit(solution)/shard_map/pallas_call | solution.py:735
  32.5 1.2 %shard_map.68 = (bf16[512,128]{1,0:T(8,128)(2,1)}, f32[9,64,64]{2,1,0:T(8,128)}, f32[9,128,256]{2,1,0:T(8,128)}) custom-call(bf16[512,128]{1,0:T(8,128)(2,1)S(1)} %get-tuple-element.9.refs_0_, f32[9,64,64]{2,1,0:T(8,128)S(1)} %get-tuple-element.10.refs_1_, f32[9,128,256]{2,1,0:T(8,128)S(1)} %get-tuple-element.11.refs_2_), custom_call_target="tpu_custom_call" | custom-call | tf_op jit(solution)/shard_map/pallas_call | solution.py:641

commit v4 on v3

--- a/solution.py
+++ b/solution.py
@@ -64,17 +64,18 @@
             device_id_type=MESH,
         )
 
-    @pl.loop(1, count)
-    def _(step):
-        copy_of(step, lambda peer: me).start()
-
-    def finish():
-        @pl.loop(1, count)
+    def start(low=1, high=count):
+        @pl.loop(low, high)
+        def _(step):
+            copy_of(step, lambda peer: me).start()
+
+    def finish(low=1, high=count):
+        @pl.loop(low, high)
         def _(step):
             copy_of(step, lambda peer: me).wait_send()
             copy_of(step, lambda peer: peer).wait_recv()
 
-    return finish
+    return start, finish
 
 
 def iota(shape, dim):
@@ -102,7 +103,7 @@
     x_any, f1_any, f2_any, up_any,
     ig_out, g1_out, g2_out,
     x_in, f1, f2, up_in, x_wide, x_turned, own, edges_f, edges, from_side, from_row, from_corner, from_up,
-    tile, patches, w1, spread_one, pre, block_f, block, gathered, up_wide, up, pool_f, pool3, near3, spread,
+    tile, patches, w1, w1_down, spread_one, spread_back, f2_down, pre, block_f, block, gathered, up_wide, up, pool_f, pool3, near3, sum_two,
     blocks, landed, grad_f, grad, grad_own, rims_f, rims, rim_rows, rim_side, rim_row, rim_corner, pool_all, near_all, pool_map, near_map,
     mine_blocks, one_landed, one_part, one_parts, one_mine, one_all, g1_wide,
     load_sem, a_send, a_recv, e_send, e_recv, b_send, b_recv, c_send, c_recv,
@@ -156,6 +157,21 @@
     shape = (width, width)
     pick = (iota(shape, 1) == 4 * (iota(shape, 0) % width2) + iota(shape, 0) // width2).astype(BF)
     low_half = iota((width2, 128), 1) < channels
+    shape = (quads, quads)
+    for i in range(2):
+        target = 4 * (iota(shape, 0) % channels) + 2 * i + iota(shape, 0) // (2 * channels)
+        spread_one[pl.ds(i * quads, quads)] = (iota(shape, 1) == target).astype(BF)
+        target = 4 * (iota(shape, 1) % channels) + 2 * i + iota(shape, 1) // (2 * channels)
+        spread_back[:, pl.ds(i * quads, quads)] = (iota(shape, 0) == target).astype(BF)
+    grad_f[...] = jnp.zeros(grad_f.shape, F32)
+    rims_f[...] = jnp.zeros(rims_f.shape, F32)
+    sum_two[...] = jnp.zeros(sum_two.shape, F32)
+    for u in range(height2):
+        pool_f[u, pl.ds(0, 2)] = jnp.zeros((2, quads), F32)
+        pool_f[u, pl.ds(2 + reach, 2)] = jnp.zeros((2, quads), F32)
+    for j in range(3):
+        near3[j, 0] = jnp.zeros(near3.shape[2:], BF)
+        near3[j, height2 + 1] = jnp.zeros(near3.shape[2:], BF)
     loads[0].wait()
     x_wide[...] = x_in[...].astype(F32)
     for h in range(band):
@@ -175,7 +191,6 @@
         edges_f[0, pl.ds(h * EDGE, EDGE)] = tile[h + 1, pl.ds(EDGE, EDGE)]
         edges_f[1, pl.ds(h * EDGE, EDGE)] = tile[h + 1, pl.ds(width2, EDGE)]
     edges[...] = edges_f[:, : band * EDGE].astype(BF)
-    loads[1].wait()
 
     diagonals = (jnp.where(row > 0, 1, 0) + jnp.where(row < rows - 1, 1, 0)) * (
         jnp.where(strip > 0, 1, 0) + jnp.where(strip < strips - 1, 1, 0)
@@ -262,6 +277,7 @@
     for way in WAYS:
         clear_border(cell_kind, way)
         clear_border(rim_kind, way)
+    loads[1].wait()
     for side in range(2):
         @pl.when(there((0, (-1, 1)[side])))
         def _(side=side):
@@ -288,10 +304,8 @@
         for p in range(4):
             for k in range(4):
                 w1[pl.ds(p * channels, channels), pl.ds(i * 512 + k * 128, 128)] = table[p][k]
-    shape = (quads, quads)
-    for i in range(2):
-        target = 4 * (iota(shape, 0) % channels) + 2 * i + iota(shape, 0) // (2 * channels)
-        spread_one[pl.ds(i * quads, quads)] = (iota(shape, 1) == target).astype(BF)
+    for k in range(12):
+        w1_down[pl.ds(k * 128, 128)] = w1[:, pl.ds(k * 128, 128)].astype(F32).T.astype(BF)
 
     def widen(line):
         here = tile[line]
@@ -321,7 +335,7 @@
     windows = jnp.concatenate(
         [patches[1 + i : band - 1 + i].reshape((band - 2) * span, 512) for i in range(3)], 1
     )
-    pre[1 : band - 1] = dot(windows, w1[...], BY_LANES).reshape(band - 2, span, quads)
+    pre[1 : band - 1] = dot(windows, w1_down[...]).reshape(band - 2, span, quads)
     halves = {h: pool(h) for h in range(2, band - 2, 2)}
 
     for way in WAYS[2:]:
@@ -336,7 +350,7 @@
     windows = jnp.concatenate(
         [jnp.concatenate([patches[i], patches[band - 1 + i]], 0) for i in range(3)], 1
     )
-    ends = dot(windows, w1[...], BY_LANES)
+    ends = dot(windows, w1_down[...])
     pre[0] = ends[:span]
     pre[band - 1] = ends[span:]
     for h in (0, band - 2):
@@ -348,16 +362,12 @@
         block_f[pl.ds(u * reach, reach)] = pooled[u * span + 2 : u * span + 2 + reach]
     pooled = block_f[: band2 * reach].astype(BF)
     block[...] = pooled
-    finish = post(rows, row, far_first(rows, row), row_device, lambda peer: block, gathered, b_send, b_recv)
+    start, finish = post(rows, row, far_first(rows, row), row_device, lambda peer: block, gathered, b_send, b_recv)
+    start()
     gathered[row] = pooled
 
     for h in range(band):
         pre[h] = slope(pre[h]) * 0.25
-    grad_f[...] = jnp.zeros(grad_f.shape, F32)
-    rims_f[...] = jnp.zeros(rims_f.shape, F32)
-    for u in range(height2):
-        pool_f[u, pl.ds(0, 2)] = jnp.zeros((2, quads), F32)
-        pool_f[u, pl.ds(2 + reach, 2)] = jnp.zeros((2, quads), F32)
     for side in range(2):
         @pl.when(there((0, (-1, 1)[side])))
         def _(side=side):
@@ -369,14 +379,39 @@
         up[u, pl.ds(0, 2)] = jnp.zeros((2, filters), F32)
         up[u, pl.ds(2, width2 + 4)] = up_wide[pl.ds(u, width2 + 4, stride=height2), :]
         up[u, pl.ds(width2 + 6, 2)] = jnp.zeros((2, filters), F32)
-    pool3[0] = jnp.zeros(pool3.shape[1:], BF)
-    pool3[height2 + 1] = jnp.zeros(pool3.shape[1:], BF)
-    for j in range(3):
-        near3[j, 0] = jnp.zeros(near3.shape[2:], BF)
-        near3[j, height2 + 1] = jnp.zeros(near3.shape[2:], BF)
     loads[3].wait()
-    finish()
-
+    for t in range(9):
+        f2_down[t // 3, pl.ds(t % 3 * quads, quads)] = f2[t].astype(F32).T.astype(BF)
+
+    half, bands = height2 // 2, rows // 2
+    near_band = jnp.where(row < bands, 0, bands)
+    far_band = bands - near_band
+
+    def forward(band_at):
+        at = band_at * band2
+        for d in range(half):
+            k = d % band2
+            pool_f[at + d, pl.ds(2, reach)] = gathered[band_at + d // band2].astype(F32)[
+                k * reach : (k + 1) * reach
+            ]
+            wide = pool_f[at + d]
+            pool3[at + d, :, pl.ds(0, quads)] = pltpu.roll(wide, 1, 0).astype(BF)
+            pool3[at + d, :, pl.ds(quads, quads)] = wide.astype(BF)
+            pool3[at + d, :, pl.ds(2 * quads, quads)] = pltpu.roll(wide, span - 1, 0).astype(BF)
+            spot = pl.multiple_of((at + d) * width2, width2)
+            pool_all[strip, pl.ds(spot, width2)] = wide[EDGE : EDGE + width2].astype(BF)
+        windows = pool3[pl.ds(at, half)].reshape(half * span, 3 * quads)
+        if filters % 128 == 0:
+            sums = dot(windows, jnp.concatenate([f2_down[i] for i in range(3)], 1))
+            sums = [sums[:, i * filters : (i + 1) * filters] for i in range(3)]
+        else:
+            sums = [dot(windows, f2_down[i]) for i in range(3)]
+        for i in range(3):
+            sum_two[pl.ds(at + 2 - i, half)] += sums[i].reshape(half, span, filters)
+
+    finish(bands + 1, rows)
+    forward(near_band)
+    finish(1, bands + 1)
     def across(source, table, send_sem, recv_sem, step):
         return pltpu.make_async_remote_copy(
             src_ref=source,
@@ -431,42 +466,39 @@
                 slot = column * pairs + lax.rem(pair + other, pairs)
                 arrival(table, send_sem, recv_sem, slot).wait_recv()
 
-    for u in range(height2):
-        r, k = divmod(u, band2)
-        pool_f[u, pl.ds(2, reach)] = gathered[r].astype(F32)[k * reach : (k + 1) * reach]
-        wide = pool_f[u]
-        pool3[u + 1, :, pl.ds(0, quads)] = pltpu.roll(wide, 1, 0).astype(BF)
-        pool3[u + 1, :, pl.ds(quads, quads)] = wide.astype(BF)
-        pool3[u + 1, :, pl.ds(2 * quads, quads)] = pltpu.roll(wide, span - 1, 0).astype(BF)
-        pool_all[strip, pl.ds(u * width2, width2)] = wide[EDGE : EDGE + width2].astype(BF)
+    forward(far_band)
     pool_sems = (p_send, p_on, p_recv)
     share(pool_all, *pool_sems)
     spots = height2 * span
-    windows = jnp.concatenate([pool3[i : i + height2].reshape(spots, 3 * quads) for i in range(3)], 1)
-    kernel = jnp.concatenate([f2[t] for t in range(9)], 1)
-    pre_two = dot(windows, kernel, BY_LANES)
+    pre_two = sum_two[1 : height2 + 1].reshape(spots, filters)
     near = up[0:height2].reshape(spots, filters) * slope(pre_two)
     near3[0, 1 : height2 + 1] = pltpu.roll(near, spots - 1, 0).astype(BF).reshape(height2, span, filters)
     near3[1, 1 : height2 + 1] = near.astype(BF).reshape(height2, span, filters)
     near3[2, 1 : height2 + 1] = pltpu.roll(near, 1, 0).astype(BF).reshape(height2, span, filters)
-    total = jnp.zeros((spots, quads), F32)
-    if filters % 128 == 0:
-        windows = [near3[j, 2 - i : 2 - i + height2].reshape(spots, filters) for i in range(3) for j in range(3)]
-        total = dot(jnp.concatenate(windows, 1), f2[...].reshape(9 * filters, quads))
-    else:
-        for t in range(9):
-            i, j = divmod(t, 3)
-            total += dot(near3[j, 2 - i : 2 - i + height2].reshape(spots, filters), f2[t])
-    spread[...] = total.reshape(height2, span, quads)
-
-    def fill(peer):
-        for k in range(band2):
-            cell = spread[peer * band2 + k]
-            blocks[peer, pl.ds(k * width2, width2)] = cell[EDGE : EDGE + width2].astype(BF)
-
-    for peer in range(rows):
-        fill(peer)
-    finish = post(rows, row, far_first(rows, row), row_device, lambda peer: blocks.at[peer], landed, c_send, c_recv)
+
+    def backward(band_at):
+        at = band_at * band2
+        windows = [
+            near3[j, pl.ds(at + 2 - i, half)].reshape(half * span, filters) for i in range(3) for j in range(3)
+        ]
+        if filters % 128 == 0:
+            total = dot(jnp.concatenate(windows, 1), f2[...].reshape(9 * filters, quads))
+        else:
+            total = jnp.zeros((half * span, quads), F32)
+            for t in range(9):
+                total += dot(windows[t], f2[t])
+        for d in range(half):
+            blocks[band_at + d // band2, pl.ds(d % band2 * width2, width2)] = total[
+                d * span + EDGE : d * span + EDGE + width2
+            ].astype(BF)
+
+    start, finish = post(
+        rows, row, far_first(rows, row), row_device, lambda peer: blocks.at[peer], landed, c_send, c_recv
+    )
+    backward(far_band)
+    start(1, bands + 1)
+    backward(near_band)
+    start(bands + 1, rows)
     landed[row] = blocks[row]
     for u in range(height2):
         near_all[strip, pl.ds(u * width2, width2)] = near[
@@ -474,12 +506,10 @@
         ].astype(BF)
     near_sems = (n_send, n_on, n_recv)
     share(near_all, *near_sems)
-    pass_on(pool_all, *pool_sems)
     finish()
     parts = total_of(rows, landed).astype(BF)
-    parts = dot(parts, spread_one[...], BY_LANES)
-
-    pass_on(near_all, *near_sems)
+    parts = dot(parts, spread_back[...])
+
     for h in range(band):
         k, i = h // 4, (h // 2) % 2
         body = parts[k * width2 : (k + 1) * width2, i * quads : (i + 1) * quads] * pre[h, mid]
@@ -519,9 +549,12 @@
         if stop - start < piece:
             begin = max(stop - start, 0)
             mine_blocks[s, pl.ds(begin, piece - begin)] = jnp.zeros((piece - begin, 128), BF)
-    finish = post(strips, strip, around(strips, strip), strip_device, lambda peer: mine_blocks.at[peer], one_landed, d1_send, d1_recv)
+    start, finish = post(strips, strip, around(strips, strip), strip_device, lambda peer: mine_blocks.at[peer], one_landed, d1_send, d1_recv)
+    start()
     one_landed[strip] = mine_blocks[strip]
 
+    pass_on(pool_all, *pool_sems)
+    pass_on(near_all, *near_sems)
     settle(pool_all, *pool_sems)
     settle(near_all, *near_sems)
     near_map[0] = jnp.zeros(near_map.shape[1:], BF)
@@ -562,12 +595,11 @@
             def _(step):
                 g2_out[3 * i : 3 * i + 3] += filter_taps(i, step)
 
-    filter_gradient(0)
-
     finish()
     part = total_of(strips, one_landed).astype(BF)
     one_part[...] = part
-    finish = post(rows, row, far_first(rows, row), row_device, lambda peer: one_part, one_parts, d2_send, d2_recv)
+    start, finish = post(rows, row, far_first(rows, row), row_device, lambda peer: one_part, one_parts, d2_send, d2_recv)
+    start()
     one_parts[row] = part
 
     for way in WAYS:
@@ -602,11 +634,13 @@
         )
     ig_out[...] = x_wide[...].astype(BF)
 
+    filter_gradient(0)
     filter_gradient(1)
     finish()
     part = total_of(rows, one_parts).astype(BF)
     one_mine[...] = part
-    finish = post(strips, strip, around(strips, strip), strip_device, lambda peer: one_mine, one_all, d3_send, d3_recv)
+    start, finish = post(strips, strip, around(strips, strip), strip_device, lambda peer: one_mine, one_all, d3_send, d3_recv)
+    start()
     one_all[strip] = part
     filter_gradient(2)
     for way in WAYS:
@@ -680,7 +714,10 @@
         v((band + 3, span, quads), F32),
         v((band + 2, span, 512)),
         v((quads, 3 * 512)),
+        v((3 * 512, quads)),
         v((2 * quads, quads)),
+        v((quads, 2 * quads)),
+        v((3, 3 * quads, filters)),
         v((band + 1, span, quads), F32),
         v((band2 * (width2 + 4) + 8, quads), F32),
         v((band2 * (width2 + 4), quads)),
@@ -688,9 +725,9 @@
         v((span * height2, filters), F32),
         v((height2 + 1, span, filters), F32),
         v((height2 + 1, span, quads), F32),
-        v((height2 + 2, span, 3 * quads)),
+        v((height2, span, 3 * quads)),
         v((3, height2 + 2, span, filters)),
-        v((height2, span, quads), F32),
+        v((height2 + 2, span, filters), F32),
         v((rows, spots, quads)),
         v((rows, spots, quads)),
         v((band + 3, span, quads), F32),

time: 33.9 us -> 32.5 us (0.959)
  Pallas kernels: 33.1 us -> 31.7 us
    pallas_call x1, Pallas kernels: 31.9 us -> 30.5 us  [local(): pl.pallas_call(functools.partial(whole_kernel, rows, strips, band, height...]
where the time goes in v4:
time: 32.5 us; the launch traced here: 32.4 us
  Pallas kernels  31.7 us (98%)
  between operations  0.64 us (2%)
    pallas_call x1, Pallas kernels, local(): pl.pallas_call(functools.partial(whole_kernel, rows, strips, band, height...  30.5 us
    pallas_call x1, Pallas kernels, write_out(): pl.pallas_call(write_kernel, out_shape=tuple((jax.ShapeDtypeStruct(a.shap...  1.18 us

profile of v4, /device:TPU:0, one launch (start us, length us, event | category | flops | bytes accessed | tf_op | source)
XLA Modules:
  0.0 32.4 jit_solution(3227723096118856217)
XLA Ops:
  0.6 30.5 %shard_map.67 = (bf16[512,128]{1,0:T(8,128)(2,1)S(1)}, f32[9,64,64]{2,1,0:T(8,128)S(1)}, f32[9,128,256]{2,1,0:T(8,128)S(1)}) custom-call(bf16[512,128]{1,0:T(8,128)(2,1)} %bitcast.19, bf16[9,64,64]{2,1,0:T(8,128)(2,1)} %bitcast.18, bf16[9,128,256]{2,1,0:T(8,128)(2,1)} %bitcast.17, bf16[256,128]{1,0:T(8,128)(2,1)} %bitcast.20), custom_call_target="tpu_custom_call" | custom-call | tf_op jit(solution)/shard_map/pallas_call | solution.py:772
  31.2 1.2 %shard_map.68 = (bf16[512,128]{1,0:T(8,128)(2,1)}, f32[9,64,64]{2,1,0:T(8,128)}, f32[9,128,256]{2,1,0:T(8,128)}) custom-call(bf16[512,128]{1,0:T(8,128)(2,1)S(1)} %get-tuple-element.9.refs_0_, f32[9,64,64]{2,1,0:T(8,128)S(1)} %get-tuple-element.10.refs_1_, f32[9,128,256]{2,1,0:T(8,128)S(1)} %get-tuple-element.11.refs_2_), custom_call_target="tpu_custom_call" | custom-call | tf_op jit(solution)/shard_map/pallas_call | solution.py:675

commit v5 on v4

--- a/solution.py
+++ b/solution.py
@@ -105,9 +105,9 @@
     x_in, f1, f2, up_in, x_wide, x_turned, own, edges_f, edges, from_side, from_row, from_corner, from_up,
     tile, patches, w1, w1_down, spread_one, spread_back, f2_down, pre, block_f, block, gathered, up_wide, up, pool_f, pool3, near3, sum_two,
     blocks, landed, grad_f, grad, grad_own, rims_f, rims, rim_rows, rim_side, rim_row, rim_corner, pool_all, near_all, pool_map, near_map,
-    mine_blocks, one_landed, one_part, one_parts, one_mine, one_all, g1_wide,
+    mine_blocks, one_landed, one_part, one_all,
     load_sem, a_send, a_recv, e_send, e_recv, b_send, b_recv, c_send, c_recv,
-    d1_send, d1_recv, d2_send, d2_recv, d3_send, d3_recv,
+    d1_send, d1_recv, d2_send, d2_recv,
     p_send, p_on, p_recv, n_send, n_on, n_recv,
 ):
     row, strip = place()
@@ -135,6 +135,7 @@
         return (a >= 0) & (a < rows) & (b >= 0) & (b < strips)
 
     barrier = pltpu.get_barrier_semaphore()
+    everyone = rows * strips
     for step in range(1, rows):
         pl.semaphore_signal(barrier, inc=1, device_id=row_device(lax.rem(row + step, rows)), device_id_type=MESH)
     for step in range(1, strips):
@@ -539,19 +540,96 @@
         cz = cut(i, 1, 1) + cut(i, 3, 3)
         halves.append(ab + jnp.where(low, za, bc))
         ends.append(cz + bc)
-    packed = halves + [jnp.where(low, ends[0], pltpu.roll(ends[1], 64, 1)), jnp.where(low, ends[2], 0.0)]
-    packed = jnp.concatenate(packed, 0).astype(BF)
-    piece = mine_blocks.shape[1]
-    for s in range(strips):
-        start, stop = s * piece, min((s + 1) * piece, packed.shape[0])
-        if stop > start:
-            mine_blocks[s, pl.ds(0, stop - start)] = packed[start:stop]
-        if stop - start < piece:
-            begin = max(stop - start, 0)
-            mine_blocks[s, pl.ds(begin, piece - begin)] = jnp.zeros((piece - begin, 128), BF)
-    start, finish = post(strips, strip, around(strips, strip), strip_device, lambda peer: mine_blocks.at[peer], one_landed, d1_send, d1_recv)
-    start()
-    one_landed[strip] = mine_blocks[strip]
+    short = channels // 2
+    last = jnp.where(low[:short], ends[2][:short], pltpu.roll(ends[2][short:], 64, 1))
+    packed = halves + [jnp.where(low, ends[0], pltpu.roll(ends[1], 64, 1)), last]
+    packed = jnp.concatenate(packed, 0)
+    owners, piece = mine_blocks.shape[:2]
+    for o in range(owners):
+        some = packed[o * piece : (o + 1) * piece]
+        if some.shape[0] < piece:
+            some = jnp.concatenate([some, jnp.zeros((piece - some.shape[0], 128), F32)], 0)
+        mine_blocks[o] = some.astype(BF)
+
+    me = row * strips + strip
+    my_piece = strip * rows + row
+    owning = my_piece < owners
+
+    def target(step):
+        z, s = step // strips, step % strips
+        return jnp.where(row < rows // 2, rows - 1 - z, z), lax.rem(strip + strips - 1 - s, strips)
+
+    def to_owner(step, arriving=False):
+        r, s = target(step)
+        other = r * strips + s
+        return pltpu.make_async_remote_copy(
+            src_ref=mine_blocks.at[my_piece if arriving else s * rows + r],
+            dst_ref=one_landed.at[other if arriving else me],
+            send_sem=d1_send.at[step],
+            recv_sem=d1_recv.at[other if arriving else me],
+            device_id=device_at(r, s),
+            device_id_type=MESH,
+        )
+
+    def from_owner(step, arriving=False):
+        r, s = target(step)
+        slot = s * rows + r if arriving else my_piece
+        return pltpu.make_async_remote_copy(
+            src_ref=one_part,
+            dst_ref=one_all.at[slot],
+            send_sem=d2_send.at[step],
+            recv_sem=d2_recv.at[slot],
+            device_id=device_at(r, s),
+            device_id_type=MESH,
+        )
+
+    def each_other(action):
+        def one(step):
+            r, s = target(step)
+
+            @pl.when(r * strips + s != me)
+            def _():
+                action(step, s * rows + r < owners)
+
+        if everyone > 16:
+            pl.loop(0, everyone)(one)
+        else:
+            for step in range(everyone):
+                one(step)
+
+    def send_out(step, owner):
+        @pl.when(owner)
+        def _():
+            to_owner(step).start()
+
+    def settle_out(step, owner):
+        @pl.when(owner)
+        def _():
+            to_owner(step).wait_send()
+
+        @pl.when(owning)
+        def _():
+            to_owner(step, True).wait_recv()
+
+    def send_back(step, owner):
+        @pl.when(owning)
+        def _():
+            from_owner(step).start()
+
+    def settle_back(step, owner):
+        @pl.when(owning)
+        def _():
+            from_owner(step).wait_send()
+
+        @pl.when(owner)
+        def _():
+            from_owner(step, True).wait_recv()
+
+    each_other(send_out)
+
+    @pl.when(owning)
+    def _():
+        one_landed[me] = mine_blocks[my_piece]
 
     pass_on(pool_all, *pool_sems)
     pass_on(near_all, *near_sems)
@@ -594,13 +672,6 @@
             @pl.loop(1, steps)
             def _(step):
                 g2_out[3 * i : 3 * i + 3] += filter_taps(i, step)
-
-    finish()
-    part = total_of(strips, one_landed).astype(BF)
-    one_part[...] = part
-    start, finish = post(rows, row, far_first(rows, row), row_device, lambda peer: one_part, one_parts, d2_send, d2_recv)
-    start()
-    one_parts[row] = part
 
     for way in WAYS:
         end_border(rim_kind, way)
@@ -634,15 +705,22 @@
         )
     ig_out[...] = x_wide[...].astype(BF)
 
-    filter_gradient(0)
-    filter_gradient(1)
-    finish()
-    part = total_of(rows, one_parts).astype(BF)
-    one_mine[...] = part
-    start, finish = post(strips, strip, around(strips, strip), strip_device, lambda peer: one_mine, one_all, d3_send, d3_recv)
-    start()
-    one_all[strip] = part
-    filter_gradient(2)
+    each_other(settle_out)
+
+    @pl.when(owning)
+    def _():
+        if everyone > 16:
+            part = lax.fori_loop(
+                1, everyone, lambda i, t: t + one_landed[i].astype(F32), one_landed[0].astype(F32)
+            )
+        else:
+            part = total_of(everyone, one_landed)
+        one_part[...] = part.astype(BF)
+        one_all[my_piece] = part.astype(BF)
+
+    each_other(send_back)
+    for i in range(3):
+        filter_gradient(i)
     for way in WAYS:
         sent_border(cell_kind, way)
         sent_border(rim_kind, way)
@@ -650,14 +728,17 @@
         @pl.when(there((0, (-1, 1)[side])))
         def _(side=side):
             up_border(side).wait_send()
-    finish()
-    done = scale_one * one_all[...].astype(F32).reshape(strips * piece, 128)
+    each_other(settle_back)
+    done = scale_one * one_all[...].astype(F32).reshape(owners * piece, 128)
     rolled = pltpu.roll(done, 64, 1)
     for i in range(3):
         for j in range(3):
-            k = i if j < 2 else 3 + i // 2
-            value = done if (j if j < 2 else i % 2) == 0 else rolled
-            g1_out[3 * i + j] = value[k * channels : (k + 1) * channels, :channels]
+            at = (i if j < 2 else 3 + i // 2) * channels
+            if (i, j) == (2, 2):
+                value = jnp.concatenate([done[at : at + short], rolled[at : at + short]], 0)
+            else:
+                value = (done if (j if j < 2 else i % 2) == 0 else rolled)[at : at + channels]
+            g1_out[3 * i + j] = value[:, :channels]
 
 
 def write_kernel(*refs):
@@ -692,7 +773,9 @@
     span = width2 + 2 * EDGE
     full2 = width2 * strips
     spots = band2 * width2
-    piece = -(-5 * channels // strips // 16) * 16
+    halves = 9 * channels // 2
+    piece = -(-halves // (rows * strips) // 8) * 8
+    owners = -(-halves // piece)
 
     def v(shape, kind=BF):
         return pltpu.VMEM(shape, kind)
@@ -743,16 +826,13 @@
         v((strips, height2 * width2, filters)),
         v((height2, full2, quads)),
         v((height2 + 2, 3 * filters, full2)),
-        v((strips, piece, 128)),
-        v((strips, piece, 128)),
+        v((owners, piece, 128)),
+        v((rows * strips, piece, 128)),
         v((piece, 128)),
-        v((rows, piece, 128)),
-        v((piece, 128)),
-        v((strips, piece, 128)),
-        v((8, 128)),
+        v((owners, piece, 128)),
         pltpu.SemaphoreType.DMA((4,)),
     ]
-    scratch += sems(len(WAYS) + 2) + sems(len(WAYS)) + sems(rows) + sems(rows) + sems(strips) + sems(rows) + sems(strips)
+    scratch += sems(len(WAYS) + 2) + sems(len(WAYS)) + sems(rows) + sems(rows) + sems(rows * strips) + sems(rows * strips)
     for _ in range(2):
         scratch += [
             pltpu.SemaphoreType.DMA((cols,)),

time: 32.5 us -> 32 us (0.985)
  Pallas kernels: 31.7 us -> 31.2 us
    pallas_call x1, Pallas kernels: 30.5 us -> 30 us  [local(): pl.pallas_call(functools.partial(whole_kernel, rows, strips, band, height...]
where the time goes in v5:
time: 32 us; the launch traced here: 31.8 us
  Pallas kernels  31.2 us (98%)
  between operations  0.64 us (2%)
    pallas_call x1, Pallas kernels, local(): pl.pallas_call(functools.partial(whole_kernel, rows, strips, band, height...  30 us
    pallas_call x1, Pallas kernels, write_out(): pl.pallas_call(write_kernel, out_shape=tuple((jax.ShapeDtypeStruct(a.shap...  1.18 us

profile of v5, /device:TPU:0, one launch (start us, length us, event | category | flops | bytes accessed | tf_op | source)
XLA Modules:
  0.0 31.8 jit_solution(14584192832219163544)
XLA Ops:
  0.6 30.0 %shard_map.67 = (bf16[512,128]{1,0:T(8,128)(2,1)S(1)}, f32[9,64,64]{2,1,0:T(8,128)S(1)}, f32[9,128,256]{2,1,0:T(8,128)S(1)}) custom-call(bf16[512,128]{1,0:T(8,128)(2,1)} %bitcast.19, bf16[9,64,64]{2,1,0:T(8,128)(2,1)} %bitcast.18, bf16[9,128,256]{2,1,0:T(8,128)(2,1)} %bitcast.17, bf16[256,128]{1,0:T(8,128)(2,1)} %bitcast.20), custom_call_target="tpu_custom_call" | custom-call | tf_op jit(solution)/shard_map/pallas_call | solution.py:852
  30.6 1.2 %shard_map.68 = (bf16[512,128]{1,0:T(8,128)(2,1)}, f32[9,64,64]{2,1,0:T(8,128)}, f32[9,128,256]{2,1,0:T(8,128)}) custom-call(bf16[512,128]{1,0:T(8,128)(2,1)S(1)} %get-tuple-element.9.refs_0_, f32[9,64,64]{2,1,0:T(8,128)S(1)} %get-tuple-element.10.refs_1_, f32[9,128,256]{2,1,0:T(8,128)S(1)} %get-tuple-element.11.refs_2_), custom_call_target="tpu_custom_call" | custom-call | tf_op jit(solution)/shard_map/pallas_call | solution.py:756

commit v6 on v5

--- a/solution.py
+++ b/solution.py
@@ -50,6 +50,10 @@
         return jnp.where(me < count // 2, down, up)
 
     return peer
+
+
+def near_first(count, me):
+    return lambda step: far_first(count, me)(count - step)
 
 
 def post(count, me, order, device_of, source, landing, send_sem, recv_sem):
@@ -69,13 +73,17 @@
         def _(step):
             copy_of(step, lambda peer: me).start()
 
-    def finish(low=1, high=count):
+    def arrive(low=1, high=count):
         @pl.loop(low, high)
         def _(step):
+            copy_of(step, lambda peer: peer).wait_recv()
+
+    def sent():
+        @pl.loop(1, count)
+        def _(step):
             copy_of(step, lambda peer: me).wait_send()
-            copy_of(step, lambda peer: peer).wait_recv()
-
-    return start, finish
+
+    return start, arrive, sent
 
 
 def iota(shape, dim):
@@ -103,7 +111,7 @@
     x_any, f1_any, f2_any, up_any,
     ig_out, g1_out, g2_out,
     x_in, f1, f2, up_in, x_wide, x_turned, own, edges_f, edges, from_side, from_row, from_corner, from_up,
-    tile, patches, w1, w1_down, spread_one, spread_back, f2_down, pre, block_f, block, gathered, up_wide, up, pool_f, pool3, near3, sum_two,
+    tile, patches, inner, w1, w1_down, spread_one, spread_back, f2_down, pre, block_f, block, gathered, up_wide, up, pool_f, pool3, near3, sum_two,
     blocks, landed, grad_f, grad, grad_own, rims_f, rims, rim_rows, rim_side, rim_row, rim_corner, pool_all, near_all, pool_map, near_map,
     mine_blocks, one_landed, one_part, one_all,
     load_sem, a_send, a_recv, e_send, e_recv, b_send, b_recv, c_send, c_recv,
@@ -167,6 +175,8 @@
     grad_f[...] = jnp.zeros(grad_f.shape, F32)
     rims_f[...] = jnp.zeros(rims_f.shape, F32)
     sum_two[...] = jnp.zeros(sum_two.shape, F32)
+    for line in (0, band + 1):
+        patches[line] = jnp.zeros(patches.shape[1:], BF)
     for u in range(height2):
         pool_f[u, pl.ds(0, 2)] = jnp.zeros((2, quads), F32)
         pool_f[u, pl.ds(2 + reach, 2)] = jnp.zeros((2, quads), F32)
@@ -333,10 +343,8 @@
             tile[h + 1, side_at[side]] = edge[h * EDGE : (h + 1) * EDGE]
     for line in range(1, band + 1):
         widen(line)
-    windows = jnp.concatenate(
-        [patches[1 + i : band - 1 + i].reshape((band - 2) * span, 512) for i in range(3)], 1
-    )
-    pre[1 : band - 1] = dot(windows, w1_down[...]).reshape(band - 2, span, quads)
+    windows = jnp.concatenate([patches[i : i + band].reshape(band * span, 512) for i in range(3)], 1)
+    pre[0:band] = dot(windows, w1_down[...]).reshape(band, span, quads)
     halves = {h: pool(h) for h in range(2, band - 2, 2)}
 
     for way in WAYS[2:]:
@@ -348,12 +356,8 @@
             corner = from_corner[2 * top + side].astype(F32)
             tile[line, side_at[side]] = corner[16 - EDGE :] if top == 0 else corner[:EDGE]
         widen(line)
-    windows = jnp.concatenate(
-        [jnp.concatenate([patches[i], patches[band - 1 + i]], 0) for i in range(3)], 1
-    )
-    ends = dot(windows, w1_down[...])
-    pre[0] = ends[:span]
-    pre[band - 1] = ends[span:]
+    pre[0] += dot(patches[0], w1_down[pl.ds(0, 512)])
+    pre[band - 1] += dot(patches[band + 1], w1_down[pl.ds(1024, 512)])
     for h in (0, band - 2):
         halves[h] = pool(h)
     pooled = jnp.concatenate([halves[4 * u] + halves[4 * u + 2] for u in range(band2)], 0)
@@ -363,12 +367,18 @@
         block_f[pl.ds(u * reach, reach)] = pooled[u * span + 2 : u * span + 2 + reach]
     pooled = block_f[: band2 * reach].astype(BF)
     block[...] = pooled
-    start, finish = post(rows, row, far_first(rows, row), row_device, lambda peer: block, gathered, b_send, b_recv)
+    start, arrive, b_sent = post(
+        rows, row, near_first(rows, row), row_device, lambda peer: block, gathered, b_send, b_recv
+    )
     start()
     gathered[row] = pooled
 
     for h in range(band):
         pre[h] = slope(pre[h]) * 0.25
+    for line in range(band + 2):
+        inner[line, :, pl.ds(0, quads)] = tile[line, mid].astype(BF)
+        inner[line, :, pl.ds(quads, 128)] = tile[line, pl.ds(EDGE - 1, width2), pl.ds(quads - 128, 128)].astype(BF)
+        inner[line, :, pl.ds(quads + 128, 128)] = tile[line, pl.ds(EDGE + 1, width2), pl.ds(0, 128)].astype(BF)
     for side in range(2):
         @pl.when(there((0, (-1, 1)[side])))
         def _(side=side):
@@ -410,9 +420,9 @@
         for i in range(3):
             sum_two[pl.ds(at + 2 - i, half)] += sums[i].reshape(half, span, filters)
 
-    finish(bands + 1, rows)
+    arrive(1, rows - bands)
     forward(near_band)
-    finish(1, bands + 1)
+    arrive(rows - bands, rows)
     def across(source, table, send_sem, recv_sem, step):
         return pltpu.make_async_remote_copy(
             src_ref=source,
@@ -493,7 +503,7 @@
                 d * span + EDGE : d * span + EDGE + width2
             ].astype(BF)
 
-    start, finish = post(
+    start, arrive, c_sent = post(
         rows, row, far_first(rows, row), row_device, lambda peer: blocks.at[peer], landed, c_send, c_recv
     )
     backward(far_band)
@@ -507,7 +517,7 @@
         ].astype(BF)
     near_sems = (n_send, n_on, n_recv)
     share(near_all, *near_sems)
-    finish()
+    arrive()
     parts = total_of(rows, landed).astype(BF)
     parts = dot(parts, spread_back[...])
 
@@ -515,20 +525,17 @@
         k, i = h // 4, (h // 2) % 2
         body = parts[k * width2 : (k + 1) * width2, i * quads : (i + 1) * quads] * pre[h, mid]
         grad_f[h + 1, mid] = body
-        grad_own[h] = grad_f[h + 1].astype(BF)
+        grad_own[pl.ds(h * width2, width2)] = body.astype(BF)
         rims_f[0, pl.ds(h, 1)] = body[:1]
         rims_f[1, pl.ds(h, 1)] = body[width2 - 1 :]
         if h in (0, band - 1):
             rim_rows[h // (band - 1)] = body.astype(BF)
-    rims[...] = rims_f[...].astype(BF)
-    for way in WAYS:
-        start_border(rim_kind, way)
 
     low = iota((channels, 128), 1) < channels
     halves, ends = [], []
     own_spots = band * span
-    windows = jnp.concatenate([patches[i : i + band].reshape(own_spots, 512) for i in range(3)], 1)
-    taps = dot(grad_own[...].reshape(own_spots, quads), windows, BY_ROWS)
+    windows = jnp.concatenate([inner[i : i + band].reshape(band * width2, 512) for i in range(3)], 1)
+    taps = dot(grad_own[...], windows, BY_ROWS)
 
     def cut(i, p, k):
         return taps[p * channels : (p + 1) * channels, i * 512 + k * 128 : i * 512 + (k + 1) * 128]
@@ -552,8 +559,16 @@
         mine_blocks[o] = some.astype(BF)
 
     me = row * strips + strip
-    my_piece = strip * rows + row
-    owning = my_piece < owners
+    low_row = rows // 2 - 1
+
+    def piece_of(r, s):
+        return 2 * s + r - low_row
+
+    def owns(r, s):
+        return (r >= low_row) & (r <= low_row + 1) & (piece_of(r, s) < owners)
+
+    my_piece = piece_of(row, strip)
+    owning = owns(row, strip)
 
     def target(step):
         z, s = step // strips, step % strips
@@ -563,7 +578,7 @@
         r, s = target(step)
         other = r * strips + s
         return pltpu.make_async_remote_copy(
-            src_ref=mine_blocks.at[my_piece if arriving else s * rows + r],
+            src_ref=mine_blocks.at[my_piece if arriving else piece_of(r, s)],
             dst_ref=one_landed.at[other if arriving else me],
             send_sem=d1_send.at[step],
             recv_sem=d1_recv.at[other if arriving else me],
@@ -573,7 +588,7 @@
 
     def from_owner(step, arriving=False):
         r, s = target(step)
-        slot = s * rows + r if arriving else my_piece
+        slot = piece_of(r, s) if arriving else my_piece
         return pltpu.make_async_remote_copy(
             src_ref=one_part,
             dst_ref=one_all.at[slot],
@@ -589,7 +604,7 @@
 
             @pl.when(r * strips + s != me)
             def _():
-                action(step, s * rows + r < owners)
+                action(step, owns(r, s))
 
         if everyone > 16:
             pl.loop(0, everyone)(one)
@@ -631,8 +646,27 @@
     def _():
         one_landed[me] = mine_blocks[my_piece]
 
+    rims[...] = rims_f[...].astype(BF)
+    for way in WAYS:
+        start_border(rim_kind, way)
+
     pass_on(pool_all, *pool_sems)
     pass_on(near_all, *near_sems)
+    each_other(settle_out)
+
+    @pl.when(owning)
+    def _():
+        if everyone > 16:
+            part = lax.fori_loop(
+                1, everyone, lambda i, t: t + one_landed[i].astype(F32), one_landed[0].astype(F32)
+            )
+        else:
+            part = total_of(everyone, one_landed)
+        one_part[...] = part.astype(BF)
+        one_all[my_piece] = part.astype(BF)
+
+    each_other(send_back)
+
     settle(pool_all, *pool_sems)
     settle(near_all, *near_sems)
     near_map[0] = jnp.zeros(near_map.shape[1:], BF)
@@ -672,6 +706,9 @@
             @pl.loop(1, steps)
             def _(step):
                 g2_out[3 * i : 3 * i + 3] += filter_taps(i, step)
+
+    for i in range(3):
+        filter_gradient(i)
 
     for way in WAYS:
         end_border(rim_kind, way)
@@ -705,22 +742,8 @@
         )
     ig_out[...] = x_wide[...].astype(BF)
 
-    each_other(settle_out)
-
-    @pl.when(owning)
-    def _():
-        if everyone > 16:
-            part = lax.fori_loop(
-                1, everyone, lambda i, t: t + one_landed[i].astype(F32), one_landed[0].astype(F32)
-            )
-        else:
-            part = total_of(everyone, one_landed)
-        one_part[...] = part.astype(BF)
-        one_all[my_piece] = part.astype(BF)
-
-    each_other(send_back)
-    for i in range(3):
-        filter_gradient(i)
+    b_sent()
+    c_sent()
     for way in WAYS:
         sent_border(cell_kind, way)
         sent_border(rim_kind, way)
@@ -774,7 +797,7 @@
     full2 = width2 * strips
     spots = band2 * width2
     halves = 9 * channels // 2
-    piece = -(-halves // (rows * strips) // 8) * 8
+    piece = -(-halves // (2 * strips) // 8) * 8
     owners = -(-halves // piece)
 
     def v(shape, kind=BF):
@@ -796,6 +819,7 @@
         v((2, 2 * height2, filters)),
         v((band + 3, span, quads), F32),
         v((band + 2, span, 512)),
+        v((band + 2, width2, 512)),
         v((quads, 3 * 512)),
         v((3 * 512, quads)),
         v((2 * quads, quads)),
@@ -815,7 +839,7 @@
         v((rows, spots, quads)),
         v((band + 3, span, quads), F32),
         v((band + 2, span, quads)),
-        v((band, span, quads)),
+        v((band * width2, quads)),
         v((2, 16, quads), F32),
         v((2, 16, quads)),
         v((2, width2, quads)),

time: 32 us -> 30.6 us (0.956)
  Pallas kernels: 31.2 us -> 29.9 us
    pallas_call x1, Pallas kernels: 30 us -> 28.7 us  [local(): pl.pallas_call(functools.partial(whole_kernel, rows, strips, band, height...]
where the time goes in v6:
time: 30.6 us; the launch traced here: 30.5 us
  Pallas kernels  29.9 us (98%)
  between operations  0.64 us (2%)
    pallas_call x1, Pallas kernels, local(): pl.pallas_call(functools.partial(whole_kernel, rows, strips, band, height...  28.7 us
    pallas_call x1, Pallas kernels, write_out(): pl.pallas_call(write_kernel, out_shape=tuple((jax.ShapeDtypeStruct(a.shap...  1.18 us

profile of v6, /device:TPU:0, one launch (start us, length us, event | category | flops | bytes accessed | tf_op | source)
XLA Modules:
  0.0 30.5 jit_solution(6027265710010147848)
XLA Ops:
  0.6 28.7 %shard_map.67 = (bf16[512,128]{1,0:T(8,128)(2,1)S(1)}, f32[9,64,64]{2,1,0:T(8,128)S(1)}, f32[9,128,256]{2,1,0:T(8,128)S(1)}) custom-call(bf16[512,128]{1,0:T(8,128)(2,1)} %bitcast.19, bf16[9,64,64]{2,1,0:T(8,128)(2,1)} %bitcast.18, bf16[9,128,256]{2,1,0:T(8,128)(2,1)} %bitcast.17, bf16[256,128]{1,0:T(8,128)(2,1)} %bitcast.20), custom_call_target="tpu_custom_call" | custom-call | tf_op jit(solution)/shard_map/pallas_call | solution.py:876
  29.3 1.2 %shard_map.68 = (bf16[512,128]{1,0:T(8,128)(2,1)}, f32[9,64,64]{2,1,0:T(8,128)}, f32[9,128,256]{2,1,0:T(8,128)}) custom-call(bf16[512,128]{1,0:T(8,128)(2,1)S(1)} %get-tuple-element.9.refs_0_, f32[9,64,64]{2,1,0:T(8,128)S(1)} %get-tuple-element.10.refs_1_, f32[9,128,256]{2,1,0:T(8,128)S(1)} %get-tuple-element.11.refs_2_), custom_call_target="tpu_custom_call" | custom-call | tf_op jit(solution)/shard_map/pallas_call | solution.py:779

commit v7 on v6

--- a/solution.py
+++ b/solution.py
@@ -111,7 +111,7 @@
     x_any, f1_any, f2_any, up_any,
     ig_out, g1_out, g2_out,
     x_in, f1, f2, up_in, x_wide, x_turned, own, edges_f, edges, from_side, from_row, from_corner, from_up,
-    tile, patches, inner, w1, w1_down, spread_one, spread_back, f2_down, pre, block_f, block, gathered, up_wide, up, pool_f, pool3, near3, sum_two,
+    tile, patches, inner, w1, w1_down, reorder, f2_down, pre, block_f, block, gathered, up_wide, up, pool_f, pool3, near3, sum_two,
     blocks, landed, grad_f, grad, grad_own, rims_f, rims, rim_rows, rim_side, rim_row, rim_corner, pool_all, near_all, pool_map, near_map,
     mine_blocks, one_landed, one_part, one_all,
     load_sem, a_send, a_recv, e_send, e_recv, b_send, b_recv, c_send, c_recv,
@@ -167,11 +167,10 @@
     pick = (iota(shape, 1) == 4 * (iota(shape, 0) % width2) + iota(shape, 0) // width2).astype(BF)
     low_half = iota((width2, 128), 1) < channels
     shape = (quads, quads)
-    for i in range(2):
-        target = 4 * (iota(shape, 0) % channels) + 2 * i + iota(shape, 0) // (2 * channels)
-        spread_one[pl.ds(i * quads, quads)] = (iota(shape, 1) == target).astype(BF)
-        target = 4 * (iota(shape, 1) % channels) + 2 * i + iota(shape, 1) // (2 * channels)
-        spread_back[:, pl.ds(i * quads, quads)] = (iota(shape, 0) == target).astype(BF)
+    for k in range(2):
+        inside, outside = iota(shape, 1 - k), iota(shape, k)
+        home = 4 * (inside % channels) + 2 * (inside // (2 * channels)) + inside // channels % 2
+        reorder[k] = (outside == home).astype(BF)
     grad_f[...] = jnp.zeros(grad_f.shape, F32)
     rims_f[...] = jnp.zeros(rims_f.shape, F32)
     sum_two[...] = jnp.zeros(sum_two.shape, F32)
@@ -283,7 +282,7 @@
             device_id_type=MESH,
         )
 
-    for way in WAYS:
+    for way in WAYS[2:] + WAYS[:2]:
         start_border(cell_kind, way)
     for way in WAYS:
         clear_border(cell_kind, way)
@@ -329,10 +328,10 @@
 
     def pool(h):
         total = (silu(pre[h]) + silu(pre[h + 1])) * 0.25
-        upper = total.astype(BF)
-        both = jnp.concatenate([upper, (total - upper.astype(F32)).astype(BF)], 0)
-        both = dot(both, spread_one[pl.ds((h // 2) % 2 * quads, quads)])
-        return both[:span] + both[span:]
+        left, right = total[:, :128], total[:, 128:]
+        left += pltpu.roll(left, 64, 1)
+        right += pltpu.roll(right, 64, 1)
+        return jnp.where(iota((span, 128), 1) < channels, left, right)
 
     side_at = [pl.ds(0, EDGE), pl.ds(EDGE + width2, EDGE)]
     for way in WAYS[:2]:
@@ -360,7 +359,8 @@
     pre[band - 1] += dot(patches[band + 1], w1_down[pl.ds(1024, 512)])
     for h in (0, band - 2):
         halves[h] = pool(h)
-    pooled = jnp.concatenate([halves[4 * u] + halves[4 * u + 2] for u in range(band2)], 0)
+    pooled = [jnp.concatenate([halves[4 * u], halves[4 * u + 2]], 1) for u in range(band2)]
+    pooled = jnp.concatenate(pooled, 0)
     at_col = strip * width2 - EDGE + iota((band2 * span, quads), 0) % span
     pooled = jnp.where((at_col >= 0) & (at_col < full2), pooled, 0.0)
     for u in range(band2):
@@ -391,6 +391,7 @@
         up[u, pl.ds(2, width2 + 4)] = up_wide[pl.ds(u, width2 + 4, stride=height2), :]
         up[u, pl.ds(width2 + 6, 2)] = jnp.zeros((2, filters), F32)
     loads[3].wait()
+    f2[...] = dot(f2[...].reshape(9 * filters, quads), reorder[0]).astype(BF).reshape(9, filters, quads)
     for t in range(9):
         f2_down[t // 3, pl.ds(t % 3 * quads, quads)] = f2[t].astype(F32).T.astype(BF)
 
@@ -518,12 +519,19 @@
     near_sems = (n_send, n_on, n_recv)
     share(near_all, *near_sems)
     arrive()
-    parts = total_of(rows, landed).astype(BF)
-    parts = dot(parts, spread_back[...])
+    parts = total_of(rows, landed)
+    wide = {}
+    for k in range(band2):
+        for i in range(2):
+            some = parts[k * width2 : (k + 1) * width2, i * 128 : (i + 1) * 128]
+            other = pltpu.roll(some, 64, 1)
+            wide[k, i] = jnp.concatenate(
+                [jnp.where(low_half, some, other), jnp.where(low_half, other, some)], 1
+            )
 
     for h in range(band):
         k, i = h // 4, (h // 2) % 2
-        body = parts[k * width2 : (k + 1) * width2, i * quads : (i + 1) * quads] * pre[h, mid]
+        body = wide[k, i] * pre[h, mid]
         grad_f[h + 1, mid] = body
         grad_own[pl.ds(h * width2, width2)] = body.astype(BF)
         rims_f[0, pl.ds(h, 1)] = body[:1]
@@ -571,8 +579,10 @@
     owning = owns(row, strip)
 
     def target(step):
-        z, s = step // strips, step % strips
-        return jnp.where(row < rows // 2, rows - 1 - z, z), lax.rem(strip + strips - 1 - s, strips)
+        z, s = step % rows, step // rows
+        return jnp.where(row < rows // 2, rows - 1 - z, z), lax.rem(col + cols - 1 - s // pairs, cols) * pairs + lax.rem(
+            pair + pairs - 1 - s % pairs, pairs
+        )
 
     def to_owner(step, arriving=False):
         r, s = target(step)
@@ -683,8 +693,8 @@
         before = jnp.where(at_lane > 0, pltpu.roll(line, 1, 1), 0.0)
         for j, value in enumerate((after, line, before)):
             near_map[u + 1, pl.ds(j * filters, filters)] = value.astype(BF)
-        for s in range(strips):
-            pool_map[u, pl.ds(s * width2, width2)] = pool_all[s, pl.ds(at, width2)]
+        line = jnp.concatenate([pool_all[s, pl.ds(at, width2)] for s in range(strips)], 0)
+        pool_map[u] = dot(line, reorder[1]).astype(BF)
 
     chunk = max(1, 1024 // full2)
     steps = height2 // chunk
@@ -822,8 +832,7 @@
         v((band + 2, width2, 512)),
         v((quads, 3 * 512)),
         v((3 * 512, quads)),
-        v((2 * quads, quads)),
-        v((quads, 2 * quads)),
+        v((2, quads, quads)),
         v((3, 3 * quads, filters)),
         v((band + 1, span, quads), F32),
         v((band2 * (width2 + 4) + 8, quads), F32),

time: 30.6 us -> 30.6 us (level)
  no operation moved by 1% of the time
where the time goes in v7:
time: 30.6 us; the launch traced here: 30.4 us
  Pallas kernels  29.8 us (97%)
  between operations  0.64 us (2%)
    pallas_call x1, Pallas kernels, local(): pl.pallas_call(functools.partial(whole_kernel, rows, strips, band, height...  28.6 us
    pallas_call x1, Pallas kernels, write_out(): pl.pallas_call(write_kernel, out_shape=tuple((jax.ShapeDtypeStruct(a.shap...  1.18 us

profile of v7, /device:TPU:0, one launch (start us, length us, event | category | flops | bytes accessed | tf_op | source)
XLA Modules:
  0.0 30.4 jit_solution(14007307128346988896)
XLA Ops:
  0.6 28.6 %shard_map.67 = (bf16[512,128]{1,0:T(8,128)(2,1)S(1)}, f32[9,64,64]{2,1,0:T(8,128)S(1)}, f32[9,128,256]{2,1,0:T(8,128)S(1)}) custom-call(bf16[512,128]{1,0:T(8,128)(2,1)} %bitcast.19, bf16[9,64,64]{2,1,0:T(8,128)(2,1)} %bitcast.18, bf16[9,128,256]{2,1,0:T(8,128)(2,1)} %bitcast.17, bf16[256,128]{1,0:T(8,128)(2,1)} %bitcast.20), custom_call_target="tpu_custom_call" | custom-call | tf_op jit(solution)/shard_map/pallas_call | solution.py:885
  29.3 1.2 %shard_map.68 = (bf16[512,128]{1,0:T(8,128)(2,1)}, f32[9,64,64]{2,1,0:T(8,128)}, f32[9,128,256]{2,1,0:T(8,128)}) custom-call(bf16[512,128]{1,0:T(8,128)(2,1)S(1)} %get-tuple-element.9.refs_0_, f32[9,64,64]{2,1,0:T(8,128)S(1)} %get-tuple-element.10.refs_1_, f32[9,128,256]{2,1,0:T(8,128)S(1)} %get-tuple-element.11.refs_2_), custom_call_target="tpu_custom_call" | custom-call | tf_op jit(solution)/shard_map/pallas_call | solution.py:789

commit v8 on v7

--- a/solution.py
+++ b/solution.py
@@ -542,11 +542,17 @@
     low = iota((channels, 128), 1) < channels
     halves, ends = [], []
     own_spots = band * span
-    windows = jnp.concatenate([inner[i : i + band].reshape(band * width2, 512) for i in range(3)], 1)
-    taps = dot(grad_own[...], windows, BY_ROWS)
+    windows = [inner[i : i + band].reshape(band * width2, 512) for i in range(3)]
+    turned = grad_own[...].astype(F32).T.astype(BF)
+    taps = dot(turned, jnp.concatenate([window[:, :quads] for window in windows], 1))
+    outer = jnp.concatenate([turned[:channels], turned[3 * channels :]], 0)
+    outer = dot(outer, jnp.concatenate([window[:, quads:] for window in windows], 1))
 
     def cut(i, p, k):
-        return taps[p * channels : (p + 1) * channels, i * 512 + k * 128 : i * 512 + (k + 1) * 128]
+        if k < 2:
+            return taps[p * channels : (p + 1) * channels, i * quads + k * 128 : i * quads + (k + 1) * 128]
+        half = channels * (p // 3)
+        return outer[half : half + channels, i * quads + (k - 2) * 128 : i * quads + (k - 1) * 128]
 
     for i in range(3):
         bc = pltpu.roll(cut(i, 0, 0) + cut(i, 2, 1), 64, 1)
@@ -579,7 +585,7 @@
     owning = owns(row, strip)
 
     def target(step):
-        z, s = step % rows, step // rows
+        z, s = step // strips, step % strips
         return jnp.where(row < rows // 2, rows - 1 - z, z), lax.rem(col + cols - 1 - s // pairs, cols) * pairs + lax.rem(
             pair + pairs - 1 - s % pairs, pairs
         )

time: 30.6 us -> 30.5 us (level)
  no operation moved by 1% of the time
where the time goes in v8:
time: 30.5 us; the launch traced here: 30.3 us
  Pallas kernels  29.7 us (97%)
  between operations  0.64 us (2%)
    pallas_call x1, Pallas kernels, local(): pl.pallas_call(functools.partial(whole_kernel, rows, strips, band, height...  28.5 us
    pallas_call x1, Pallas kernels, write_out(): pl.pallas_call(write_kernel, out_shape=tuple((jax.ShapeDtypeStruct(a.shap...  1.18 us

profile of v8, /device:TPU:0, one launch (start us, length us, event | category | flops | bytes accessed | tf_op | source)
XLA Modules:
  0.0 30.3 jit_solution(6910548935500358672)
XLA Ops:
  0.6 28.5 %shard_map.67 = (bf16[512,128]{1,0:T(8,128)(2,1)S(1)}, f32[9,64,64]{2,1,0:T(8,128)S(1)}, f32[9,128,256]{2,1,0:T(8,128)S(1)}) custom-call(bf16[512,128]{1,0:T(8,128)(2,1)} %bitcast.19, bf16[9,64,64]{2,1,0:T(8,128)(2,1)} %bitcast.18, bf16[9,128,256]{2,1,0:T(8,128)(2,1)} %bitcast.17, bf16[256,128]{1,0:T(8,128)(2,1)} %bitcast.20), custom_call_target="tpu_custom_call" | custom-call | tf_op jit(solution)/shard_map/pallas_call | solution.py:891
  29.1 1.2 %shard_map.68 = (bf16[512,128]{1,0:T(8,128)(2,1)}, f32[9,64,64]{2,1,0:T(8,128)}, f32[9,128,256]{2,1,0:T(8,128)}) custom-call(bf16[512,128]{1,0:T(8,128)(2,1)S(1)} %get-tuple-element.9.refs_0_, f32[9,64,64]{2,1,0:T(8,128)S(1)} %get-tuple-element.10.refs_1_, f32[9,128,256]{2,1,0:T(8,128)S(1)} %get-tuple-element.11.refs_2_), custom_call_target="tpu_custom_call" | custom-call | tf_op jit(solution)/shard_map/pallas_call | solution.py:795

commit v9 on v8

--- a/solution.py
+++ b/solution.py
@@ -666,8 +666,6 @@
     for way in WAYS:
         start_border(rim_kind, way)
 
-    pass_on(pool_all, *pool_sems)
-    pass_on(near_all, *near_sems)
     each_other(settle_out)
 
     @pl.when(owning)
@@ -682,6 +680,8 @@
         one_all[my_piece] = part.astype(BF)
 
     each_other(send_back)
+    pass_on(pool_all, *pool_sems)
+    pass_on(near_all, *near_sems)
 
     settle(pool_all, *pool_sems)
     settle(near_all, *near_sems)

time: 30.5 us -> 30.5 us (level)
  no operation moved by 1% of the time
where the time goes in v9:
time: 30.5 us; the launch traced here: 30.3 us
  Pallas kernels  29.7 us (97%)
  between operations  0.64 us (2%)
    pallas_call x1, Pallas kernels, local(): pl.pallas_call(functools.partial(whole_kernel, rows, strips, band, height...  28.5 us
    pallas_call x1, Pallas kernels, write_out(): pl.pallas_call(write_kernel, out_shape=tuple((jax.ShapeDtypeStruct(a.shap...  1.18 us

profile of v9, /device:TPU:0, one launch (start us, length us, event | category | flops | bytes accessed | tf_op | source)
XLA Modules:
  0.0 30.3 jit_solution(14249780152801975758)
XLA Ops:
  0.6 28.5 %shard_map.67 = (bf16[512,128]{1,0:T(8,128)(2,1)S(1)}, f32[9,64,64]{2,1,0:T(8,128)S(1)}, f32[9,128,256]{2,1,0:T(8,128)S(1)}) custom-call(bf16[512,128]{1,0:T(8,128)(2,1)} %bitcast.19, bf16[9,64,64]{2,1,0:T(8,128)(2,1)} %bitcast.18, bf16[9,128,256]{2,1,0:T(8,128)(2,1)} %bitcast.17, bf16[256,128]{1,0:T(8,128)(2,1)} %bitcast.20), custom_call_target="tpu_custom_call" | custom-call | tf_op jit(solution)/shard_map/pallas_call | solution.py:891
  29.1 1.2 %shard_map.68 = (bf16[512,128]{1,0:T(8,128)(2,1)}, f32[9,64,64]{2,1,0:T(8,128)}, f32[9,128,256]{2,1,0:T(8,128)}) custom-call(bf16[512,128]{1,0:T(8,128)(2,1)S(1)} %get-tuple-element.9.refs_0_, f32[9,64,64]{2,1,0:T(8,128)S(1)} %get-tuple-element.10.refs_1_, f32[9,128,256]{2,1,0:T(8,128)S(1)} %get-tuple-element.11.refs_2_), custom_call_target="tpu_custom_call" | custom-call | tf_op jit(solution)/shard_map/pallas_call | solution.py:795

commit v10 on v8

--- a/solution.py
+++ b/solution.py
@@ -160,7 +160,7 @@
         pltpu.make_async_copy(source, target, load_sem.at[n])
         for n, (source, target) in enumerate([(x_any, x_in), (up_any, up_in), (f1_any, f1), (f2_any, f2)])
     ]
-    for load in loads:
+    for load in loads[:3]:
         load.start()
 
     shape = (width, width)
@@ -183,6 +183,7 @@
         near3[j, 0] = jnp.zeros(near3.shape[2:], BF)
         near3[j, height2 + 1] = jnp.zeros(near3.shape[2:], BF)
     loads[0].wait()
+    loads[3].start()
     x_wide[...] = x_in[...].astype(F32)
     for h in range(band):
         line = x_wide[pl.ds(h, channels, stride=band), :].astype(BF)

time: 30.5 us -> 30.5 us (level)
  no operation moved by 1% of the time
where the time goes in v10:
time: 30.5 us; the launch traced here: 30.3 us
  Pallas kernels  29.7 us (97%)
  between operations  0.64 us (2%)
    pallas_call x1, Pallas kernels, local(): pl.pallas_call(functools.partial(whole_kernel, rows, strips, band, height...  28.5 us
    pallas_call x1, Pallas kernels, write_out(): pl.pallas_call(write_kernel, out_shape=tuple((jax.ShapeDtypeStruct(a.shap...  1.18 us

profile of v10, /device:TPU:0, one launch (start us, length us, event | category | flops | bytes accessed | tf_op | source)
XLA Modules:
  0.0 30.3 jit_solution(7083827376281755014)
XLA Ops:
  0.6 28.5 %shard_map.67 = (bf16[512,128]{1,0:T(8,128)(2,1)S(1)}, f32[9,64,64]{2,1,0:T(8,128)S(1)}, f32[9,128,256]{2,1,0:T(8,128)S(1)}) custom-call(bf16[512,128]{1,0:T(8,128)(2,1)} %bitcast.19, bf16[9,64,64]{2,1,0:T(8,128)(2,1)} %bitcast.18, bf16[9,128,256]{2,1,0:T(8,128)(2,1)} %bitcast.17, bf16[256,128]{1,0:T(8,128)(2,1)} %bitcast.20), custom_call_target="tpu_custom_call" | custom-call | tf_op jit(solution)/shard_map/pallas_call | solution.py:892
  29.1 1.2 %shard_map.68 = (bf16[512,128]{1,0:T(8,128)(2,1)}, f32[9,64,64]{2,1,0:T(8,128)}, f32[9,128,256]{2,1,0:T(8,128)}) custom-call(bf16[512,128]{1,0:T(8,128)(2,1)S(1)} %get-tuple-element.9.refs_0_, f32[9,64,64]{2,1,0:T(8,128)S(1)} %get-tuple-element.10.refs_1_, f32[9,128,256]{2,1,0:T(8,128)S(1)} %get-tuple-element.11.refs_2_), custom_call_target="tpu_custom_call" | custom-call | tf_op jit(solution)/shard_map/pallas_call | solution.py:796
